TPU v7x, 512 devices: a whole 4x8x8 slice. The times are simulated.
512 devices in a mesh: wide: 128 (over z, y, core), mp: 4 (over x).
Axes of the slice: x: 4, y: 8, z: 8, core: 2. Of those that a mesh axis runs over, the one named last changes fastest.
Arguments:
- passage_states: bfloat16 [32768, 8192], P('wide', 'mp')
- norm_gain: float32 [8192], P('mp'), may hold values from 0.1 to 1.9
- proj_weight: bfloat16 [8192, 1024], P('mp', 'wide'), may hold values from -0.0625 to 0.0625
- query_states: bfloat16 [32768, 4096], P('wide', 'mp')
- self_keyvals: bfloat16 [32768, 1024], P('wide', 'mp')
- output_grads: bfloat16 [32768, 4096], P('wide', 'mp'), may hold values from -6 to 6
- passage_ids: int32 [256, 32], P('wide'), may hold values from -1 to 2047, as said below
- passage_counts: int32 [256], P('wide'), may hold values from 16 to 32, as said below
Outputs:
- state_grads: bfloat16 [32768, 8192], P('wide', 'mp')
- gain_grads: float32 [8192], P('mp')
- query_gradient: float32 [32768, 4096], P('wide', 'mp')
- self_keyval_grads: float32 [32768, 1024], P('wide', 'mp')
Inputs may be any that keep to these rules, and one draw needn't show every extreme that they name: `passage_ids`: passage p lives on index p // 16 of wide. Row q names distinct passages in its first passage_counts[q] entries and holds -1 after them. The 2 questions of one index of wide name distinct passages and together read at most 1 passages that live on any one index of wide; that bound is reached in every draw. `passage_counts`: some question reads 32 passages in every draw.
All inputs are finite; a program needn't handle non-finite values.
Results may differ from a plain program's by a relative error of at most 0.012.
Values may be sent and summed in bfloat16 or wider, within the bound.
No kernel may reach another device: no remote copies, remote signals or barrier semaphores. Data moves between devices by JAX's collectives and lax.ppermute only.
A program may use at most 64 MiB of HBM per device.

v0:
```python
import math

import jax
import jax.numpy as jnp
from jax import lax
from jax.sharding import PartitionSpec as P

D = 8192
MROWS = 16


epsilon = 1e-05


def attend(query_block, grad_block, memory_block, self_block, live_count):
    head_dim = query_block.shape[-1]
    score_scale = 1.0 / math.sqrt(head_dim)
    mem_total = memory_block.shape[0]
    seq_len = query_block.shape[0]
    memory_key_rows = jnp.concatenate(
        [memory_block[:, :head_dim], self_block[:, :head_dim]], axis=0
    )
    memory_value_rows = jnp.concatenate(
        [memory_block[:, head_dim:], self_block[:, head_dim:]], axis=0
    )
    columns = jnp.arange(mem_total + seq_len)
    positions = jnp.arange(seq_len)
    allowed = jnp.where(
        columns[None, :] < mem_total,
        columns[None, :] < live_count * MROWS,
        columns[None, :] - mem_total <= positions[:, None],
    )
    score_matrix = (
        jnp.einsum("lgd,md->glm", query_block, memory_key_rows, preferred_element_type=jnp.float32)
        * score_scale
    )
    score_matrix = jnp.where(allowed[None], score_matrix, -1e30)
    score_matrix = score_matrix - jnp.max(score_matrix, -1, keepdims=True)
    exponent = jnp.exp(score_matrix)
    probabilities = exponent / jnp.sum(exponent, -1, keepdims=True)
    rounded_scores = probabilities.astype(jnp.bfloat16)
    attended_values = jnp.einsum(
        "glm,md->lgd", rounded_scores, memory_value_rows, preferred_element_type=jnp.float32
    )
    row_delta = jnp.transpose(jnp.sum(grad_block.astype(jnp.float32) * attended_values, -1), (1, 0))
    probability_gradient = jnp.einsum(
        "lgd,md->glm", grad_block, memory_value_rows, preferred_element_type=jnp.float32
    )
    score_gradient = (
        probabilities * (probability_gradient - row_delta[..., None]) * score_scale
    ).astype(jnp.bfloat16)
    query_part = jnp.einsum(
        "glm,md->lgd", score_gradient, memory_key_rows, preferred_element_type=jnp.float32
    )
    key_gradient = jnp.einsum(
        "glm,lgd->md", score_gradient, query_block, preferred_element_type=jnp.float32
    )
    value_gradient = jnp.einsum(
        "glm,lgd->md", rounded_scores, grad_block, preferred_element_type=jnp.float32
    )
    both_grads = jnp.concatenate([key_gradient, value_gradient], axis=1)
    return (
        query_part.reshape(seq_len, -1),
        both_grads[mem_total:],
        both_grads[:mem_total].astype(jnp.bfloat16),
    )


def on_device(
    passage_states,
    norm_gain,
    proj_weight,
    query_states,
    self_keyvals,
    output_grads,
    passage_ids,
    passage_counts,
):
    wide_count = lax.axis_size("wide")
    states = passage_states.astype(jnp.float32)
    squares = lax.psum(jnp.sum(states * states, 1), "mp")
    inverse_rms = lax.rsqrt(squares / D + epsilon)[:, None]
    normed = states * inverse_rms
    memory_rows = (normed * norm_gain).astype(jnp.bfloat16)
    whole_weight = lax.all_gather(proj_weight, "wide", axis=1, tiled=True)
    partial_sums = jnp.dot(memory_rows, whole_weight, preferred_element_type=jnp.float32)
    head_rows = lax.psum_scatter(partial_sums, "mp", scatter_dimension=1, tiled=True).astype(
        jnp.bfloat16
    )
    row_width = head_rows.shape[1]
    passage_count = head_rows.shape[0] // MROWS
    passage_table = head_rows.reshape(passage_count, MROWS * row_width)
    local_questions = passage_ids.shape[0]
    capacity = passage_ids.shape[1]
    request_ids = passage_ids.reshape(-1)
    list_pos = jnp.arange(capacity, dtype=jnp.int32)
    is_valid = (list_pos[None, :] < passage_counts[:, None]).reshape(-1)
    owners = jnp.where(is_valid, request_ids // passage_count, -1)
    local_rows = request_ids % passage_count
    request_total = owners.shape[0]
    request_order = jnp.arange(request_total)
    earlier = (owners[None, :] == owners[:, None]) & (
        request_order[None, :] < request_order[:, None]
    )
    slot_index = jnp.sum(earlier.astype(jnp.int32), 1)
    slot_width = request_total // min(request_total, wide_count)
    buffer_len = wide_count * slot_width
    targets = jnp.where(is_valid, owners * slot_width + slot_index, -1)
    placed = targets[:, None] == jnp.arange(buffer_len)[None, :]
    request_table = jnp.sum(jnp.where(placed, local_rows[:, None] + 1, 0), 0) - 1
    received = lax.all_to_all(
        request_table.reshape(wide_count, slot_width),
        "wide",
        split_axis=0,
        concat_axis=0,
        tiled=True,
    )
    wanted = received.reshape(-1)
    choose = (wanted[:, None] == jnp.arange(passage_count)[None, :]).astype(jnp.bfloat16)
    outgoing = jnp.dot(choose, passage_table, preferred_element_type=jnp.float32).astype(
        jnp.bfloat16
    )
    arrived = lax.all_to_all(
        outgoing.reshape(wide_count, slot_width, -1),
        "wide",
        split_axis=0,
        concat_axis=0,
        tiled=True,
    )
    placed_rows = placed.astype(jnp.bfloat16)
    gathered = jnp.dot(
        placed_rows, arrived.reshape(buffer_len, -1), preferred_element_type=jnp.float32
    ).astype(jnp.bfloat16)
    token_count = query_states.shape[0]
    seq_len = token_count // local_questions
    head_dim = row_width // 2
    head_group = query_states.shape[1] // head_dim
    query_rows = query_states.reshape(local_questions, seq_len, head_group, head_dim)
    grad_rows = output_grads.reshape(local_questions, seq_len, head_group, head_dim)
    self_rows = self_keyvals.reshape(local_questions, seq_len, row_width)
    memory = gathered.reshape(local_questions, capacity * MROWS, row_width)

    def per_question(question_items):
        return attend(*question_items)

    query_parts, self_parts, memory_parts = lax.map(
        per_question, (query_rows, grad_rows, memory, self_rows, passage_counts)
    )
    query_gradient = query_parts.reshape(token_count, head_group * head_dim)
    self_keyval_grads = self_parts.reshape(token_count, row_width)
    memory_grads = memory_parts.reshape(request_total, MROWS * row_width)
    spread_back = lax.dot_general(
        placed_rows, memory_grads, (((0,), (0,)), ((), ())), preferred_element_type=jnp.float32
    ).astype(jnp.bfloat16)
    returned = lax.all_to_all(
        spread_back.reshape(wide_count, slot_width, -1),
        "wide",
        split_axis=0,
        concat_axis=0,
        tiled=True,
    )
    summed = lax.dot_general(
        choose,
        returned.reshape(buffer_len, -1),
        (((0,), (0,)), ((), ())),
        preferred_element_type=jnp.float32,
    )
    passage_grads = summed.astype(jnp.bfloat16).reshape(passage_count * MROWS, row_width)
    all_heads = lax.all_gather(passage_grads, "mp", axis=1, tiled=True)
    row_grads = lax.dot_general(
        all_heads, whole_weight, (((1,), (1,)), ((), ())), preferred_element_type=jnp.float32
    )
    scaled_grads = row_grads * norm_gain
    gain_grads = lax.psum(jnp.sum(row_grads * normed, 0), "wide")
    row_mean = lax.psum(jnp.sum(scaled_grads * normed, 1), "mp") / D
    state_grads = (inverse_rms * (scaled_grads - normed * row_mean[:, None])).astype(jnp.bfloat16)
    return (state_grads, gain_grads, query_gradient, self_keyval_grads)


def solution(mesh):
    in_specs = (
        P("wide", "mp"),
        P("mp"),
        P("mp", "wide"),
        P("wide", "mp"),
        P("wide", "mp"),
        P("wide", "mp"),
        P("wide", None),
        P("wide"),
    )
    out_specs = (P("wide", "mp"), P("mp"), P("wide", "mp"), P("wide", "mp"))
    return jax.shard_map(
        on_device, mesh=mesh, in_specs=in_specs, out_specs=out_specs, check_vma=False
    )
```

profile of v0, /device:TPU:2, one launch (start us, length us, event | category | flops | bytes accessed | tf_op | source)
XLA Modules:
  0.0 543.8 jit_solution(9977206591443623822)
XLA Ops:
  7.9 1.5 fusion.40
  9.5 13.6 %psum.21 = f32[256]{0:T(256)S(1)} all-reduce(f32[256]{0:T(256)S(1)} %fusion.40), channel_id=1, replica_groups=mesh['wide'=128,'mp'=4] {'mp'}, use_global_device_ids=true, to_apply=%region_1.0 | all-reduce | flops 256 | bytes 2048 | tf_op jit(solution)/shard_map/psum | solution.py:81
  23.1 77.4 %all-gather.2.cloned.1.call-done = bf16[2048,1024]{0,1:T(8,128)(2,1)} async-done(((bf16[2048,8]{0,1:T(8,128)(2,1)}), bf16[2048,1024]{0,1:T(8,128)(2,1)}) %all-gather.2.cloned.1.call-update) | async-done | bytes 4194320 | tf_op jit(solution)/shard_map/all_gather | solution.py:85
  100.5 4.8 fusion.41
  107.3 10.0 %all-to-all-start = ((s32[128,1,1]{2,1,0:T(1,128)}), s32[128,1,1]{2,1,0:T(1,128)S(1)}, u32[]{:S(2)}, u32[]{:S(2)}) async-start(s32[128,1,1]{2,1,0:T(1,128)} %copy.80), calls=%async_computation | async-start | bytes 131072 | tf_op jit(solution)/shard_map/all_to_all | solution.py:111
  117.3 11.1 %all-to-all-done = s32[128,1,1]{2,1,0:T(1,128)S(1)} async-done(((s32[128,1,1]{2,1,0:T(1,128)}), s32[128,1,1]{2,1,0:T(1,128)S(1)}, u32[]{:S(2)}, u32[]{:S(2)}) %all-to-all-start) | async-done | bytes 544 | tf_op jit(solution)/shard_map/all_to_all | solution.py:111
  128.4 2.3 reduce
  132.8 1.4 reduce.1
  134.2 1.6 reshape.285
  135.8 13.4 %all-to-all-start.1 = ((bf16[128,2,2048]{2,1,0:T(2,128)(2,1)}), bf16[128,2,2048]{2,1,0:T(2,128)(2,1)S(1)}, u32[]{:S(2)}, u32[]{:S(2)}) async-start(bf16[128,2,2048]{2,1,0:T(2,128)(2,1)} %reshape.285), calls=%async_computation.2 | async-start | bytes 2097152 | tf_op jit(solution)/shard_map/all_to_all | solution.py:123
  151.0 28.3 %all-to-all-done.1 = bf16[128,2,2048]{2,1,0:T(2,128)(2,1)S(1)} async-done(((bf16[128,2,2048]{2,1,0:T(2,128)(2,1)}), bf16[128,2,2048]{2,1,0:T(2,128)(2,1)S(1)}, u32[]{:S(2)}, u32[]{:S(2)}) %all-to-all-start.1) | async-done | bytes 1048608 | tf_op jit(solution)/shard_map/all_to_all | solution.py:123
  182.7 30.4 %while.16 = (s32[]{:T(128)}, f32[2,128,1024]{2,1,0:T(8,128)}, f32[2,128,256]{2,1,0:T(8,128)}, bf16[2,512,256]{2,1,0:T(8,128)(2,1)}, bf16[2,512,256]{2,1,0:T(8,12...) while((s32[]{:T(128)}, f32[2,128,1024]{2,1,0:T(8,128)}, ...), condition=%wide.region_9.10_spmd, body=%wide.region_5.9_spmd.sunk | while | flops 1016268288 | bytes 40955756 | solution.py:146
  182.7 1.3 dynamic_slice.45
  188.7 1.9 fusion.89
  192.2 1.5 fusion.92
  203.9 1.9 fusion.89
  207.3 1.5 fusion.92
  214.9 1.4 reduce.2
  217.1 37.2 %all_to_all.16 = bf16[128,2,2048]{2,1,0:T(2,128)(2,1)S(1)} all-to-all(bf16[128,2,2048]{2,1,0:T(2,128)(2,1)S(1)} %reshape.287), channel_id=1, replica_groups=mesh['wide'=128,'mp'=4] {'wide'}, dimensions={0} | all-to-all | bytes 2097152 | tf_op jit(solution)/shard_map/all_to_all | solution.py:155
  256.6 12.8 %all_gather.7 = bf16[256,1024]{1,0:T(8,128)(2,1)S(1)} all-gather(bf16[256,256]{1,0:T(8,128)(2,1)S(1)} %reshape.275), channel_id=1, replica_groups=mesh['wide'=128,'mp'=4] {'mp'}, dimensions={1}, use_global_device_ids=true | all-gather | bytes 655360 | tf_op jit(solution)/shard_map/all_gather | solution.py:169
  269.4 3.7 fusion.39
  273.1 251.5 %psum.23 = f32[2048]{0:T(1024)} all-reduce(f32[2048]{0:T(1024)S(1)} %get-tuple-element.158), channel_id=1, replica_groups=mesh['wide'=128,'mp'=4] {'wide'}, use_global_device_ids=true, to_apply=%region_13.14 | all-reduce | flops 2048 | bytes 16384 | tf_op jit(solution)/shard_map/psum | solution.py:174
  524.6 10.9 %psum.22 = f32[256]{0:T(256)S(1)} all-reduce(f32[256]{0:T(256)S(1)} %get-tuple-element.159), channel_id=1, replica_groups=mesh['wide'=128,'mp'=4] {'mp'}, use_global_device_ids=true, to_apply=%region_11.12 | all-reduce | flops 256 | bytes 2048 | tf_op jit(solution)/shard_map/psum | solution.py:175
  535.5 1.5 fusion.38
  (115 shorter events, 35.5 us)
Async XLA Ops:
  7.2 93.3 %all-gather.2.cloned.1.call-start = ((), (), s32[]{:S(2)}) async-start(), calls=%async_computation.4 | async-start | bytes 4227072 | tf_op jit(solution)/shard_map/all_gather | solution.py:85
  7.9 122.8 %reduce-scatter.2.cloned.1.call-start = ((), (), s32[]{:S(2)}) async-start(), calls=%async_computation.5 | async-start | bytes 1310720 | tf_op jit(solution)/shard_map/reduce_scatter | solution.py:87
  23.1 82.2 %copy-start.11 = (s32[2,32]{1,0:T(2,128)S(1)}, s32[2,32]{1,0:T(2,128)}, u32[]{:S(2)}) copy-start(s32[2,32]{1,0:T(2,128)} %param.16) | copy-start | bytes 772
  107.3 21.1 %all-to-all-start = ((s32[128,1,1]{2,1,0:T(1,128)}), s32[128,1,1]{2,1,0:T(1,128)S(1)}, u32[]{:S(2)}, u32[]{:S(2)}) async-start(s32[128,1,1]{2,1,0:T(1,128)} %copy.80), calls=%async_computation | async-start | bytes 131072 | tf_op jit(solution)/shard_map/all_to_all | solution.py:111
  134.2 15.0 %copy-start.4 = (bf16[256,1024]{1,0:T(8,128)(2,1)S(1)}, bf16[256,1024]{1,0:T(8,128)(2,1)}, u32[]{:S(2)}) copy-start(bf16[256,1024]{1,0:T(8,128)(2,1)} %param.13) | copy-start | bytes 1572868
  135.8 14.3 %copy-start.5 = (bf16[256,1024]{1,0:T(8,128)(2,1)S(1)}, bf16[256,1024]{1,0:T(8,128)(2,1)}, u32[]{:S(2)}) copy-start(bf16[256,1024]{1,0:T(8,128)(2,1)} %param.15) | copy-start | bytes 1572868
  135.8 43.5 %all-to-all-start.1 = ((bf16[128,2,2048]{2,1,0:T(2,128)(2,1)}), bf16[128,2,2048]{2,1,0:T(2,128)(2,1)S(1)}, u32[]{:S(2)}, u32[]{:S(2)}) async-start(bf16[128,2,2048]{2,1,0:T(2,128)(2,1)} %reshape.285), calls=%async_computation.2 | async-start | bytes 2097152 | tf_op jit(solution)/shard_map/all_to_all | solution.py:123
  187.5 3.1 copy-start
  187.5 3.3 copy-start.3
  192.1 2.1 copy-start.1
  194.7 1.2 copy-start.6
  194.7 1.4 copy-start.9
  196.1 0.8 copy-start.7
  196.9 1.0 copy-start.10
  202.7 3.1 copy-start
  202.7 3.3 copy-start.3
  207.3 2.1 copy-start.1
  209.9 1.2 copy-start.6
  209.9 1.4 copy-start.9
  211.3 0.8 copy-start.7
  212.1 1.0 copy-start.10
  254.3 15.1 %copy-start.8 = (f32[2048]{0:T(1024)S(1)}, f32[2048]{0:T(1024)}, u32[]{:S(2)}) copy-start(f32[2048]{0:T(1024)} %param.11) | copy-start | bytes 24580
  255.3 14.1 %copy-start.2 = (bf16[256,2048]{1,0:T(8,128)(2,1)S(1)}, bf16[256,2048]{1,0:T(8,128)(2,1)}, u32[]{:S(2)}) copy-start(bf16[256,2048]{1,0:T(8,128)(2,1)} %param.10) | copy-start | bytes 3145732
Sparse Core Ops, SparseCore 0:
  11.1 89.3 all-gather.1
  105.4 23.6 reduce-scatter.1
where the time goes:
time: 545 us; the launch traced here: 544 us
  blocking collectives  326 us (60%)
  waiting for transfers between devices  117 us (21%)
  local copies, waits for them, and re-layouts  25 us (5%)
  starting transfers between devices  23.4 us (4%)
  matrix products  23.4 us (4%)
  between operations  14.2 us (3%)
  other arithmetic  12.6 us (2%)
    psum x1, blocking collectives, on_device(): gain_grads = lax.psum(jnp.sum(row_grads * normed, 0), 'wide')  251 us
    all_gather x1, waiting for transfers between devices, on_device(): whole_weight = lax.all_gather(proj_weight, 'wide', axis=1, tiled=True)  77.4 us
    all_to_all x1, blocking collectives, on_device(): lax.all_to_all(spread_back.reshape(wide_count, slot_width, -1), 'wide', s...  37.2 us
    all_to_all x1, waiting for transfers between devices, on_device(): lax.all_to_all(outgoing.reshape(wide_count, slot_width, -1), 'wide', spli...  28.3 us
    psum x1, blocking collectives, on_device(): squares = lax.psum(jnp.sum(states * states, 1), 'mp')  13.6 us
    all_to_all x1, starting transfers between devices, on_device(): lax.all_to_all(outgoing.reshape(wide_count, slot_width, -1), 'wide', spli...  13.4 us
    all_gather x1, blocking collectives, on_device(): all_heads = lax.all_gather(passage_grads, 'mp', axis=1, tiled=True)  12.8 us
    all_to_all x1, waiting for transfers between devices, on_device(): lax.all_to_all(request_table.reshape(wide_count, slot_width), 'wide', spl...  11.1 us
  transfers between devices with their start and end apart: 4, of which 3 were waited for; matrix products, arithmetic and copies ran while one was open for 1% of the time, Pallas kernels for 0%

commit v1 on v0

v1 whole, which is shorter than its diff:
```python
import math

import jax
import jax.numpy as jnp
from jax import lax
from jax.experimental import pallas as pl
from jax.experimental.pallas import tpu as pltpu
from jax.sharding import Mesh
from jax.sharding import PartitionSpec as P

D = 8192
MROWS = 16
HEAD = 128
GROUP = 8
QLEN = 128
CAP = 32
MEM = CAP * MROWS
KEYS = MEM + QLEN
N_WIDE = 128
P_DEV = 16
EPSILON = 1e-05
SCALE = 1.0 / math.sqrt(HEAD)
LOG2E = math.log2(math.e)
VMEM_LIMIT = 48 * 1024 * 1024

NT = (((1,), (1,)), ((), ()))
TN = (((0,), (0,)), ((), ()))


def dot(a, b, dims=(((1,), (0,)), ((), ()))):
    return lax.dot_general(a, b, dims, preferred_element_type=jnp.float32)


def params():
    return pltpu.CompilerParams(vmem_limit_bytes=VMEM_LIMIT)


def whole(shape):
    return pl.BlockSpec(shape, lambda *_: (0,) * len(shape))


def project_kernel(rows_ref, weight_ref, out_ref):
    out_ref[0] = dot(rows_ref[...], weight_ref[...], NT).astype(out_ref.dtype)


def project(rows, blob, dtype):
    row_total, depth = rows.shape
    heads = blob.shape[0] // (2 * HEAD)
    return pl.pallas_call(
        project_kernel,
        grid=(heads,),
        in_specs=[
            whole((row_total, depth)),
            pl.BlockSpec((2 * HEAD, depth), lambda h: (h, 0)),
        ],
        out_specs=pl.BlockSpec((1, row_total, 2 * HEAD), lambda h: (h, 0, 0)),
        out_shape=jax.ShapeDtypeStruct((heads, row_total, 2 * HEAD), dtype),
        compiler_params=params(),
        cost_estimate=pl.CostEstimate(
            flops=2 * row_total * depth * heads * 2 * HEAD, bytes_accessed=4 << 20, transcendentals=0
        ),
    )(rows, blob)


def pack_kernel(wanted_ref, parts_ref, out_ref, keyvals_ref, table_ref):
    total = parts_ref[0].astype(jnp.float32)
    for part in range(1, parts_ref.shape[0]):
        total = total + parts_ref[part].astype(jnp.float32)
    total = total.reshape(P_DEV, MROWS, 2 * HEAD)
    keyvals_ref[...] = total
    table_ref[...] = total.astype(jnp.bfloat16)
    for slot in range(N_WIDE):
        out_ref[slot] = table_ref[jnp.maximum(wanted_ref[slot], 0)]


def pack(wanted, parts):
    table = (P_DEV, MROWS, 2 * HEAD)
    outgoing = (N_WIDE, MROWS, 2 * HEAD)
    return pl.pallas_call(
        pack_kernel,
        grid_spec=pltpu.PrefetchScalarGridSpec(
            num_scalar_prefetch=1,
            grid=(1,),
            in_specs=[whole(parts.shape)],
            out_specs=[whole(outgoing), whole(table)],
            scratch_shapes=[pltpu.VMEM(table, jnp.bfloat16)],
        ),
        out_shape=[
            jax.ShapeDtypeStruct(outgoing, jnp.bfloat16),
            jax.ShapeDtypeStruct(table, jnp.float32),
        ],
        compiler_params=params(),
        cost_estimate=pl.CostEstimate(flops=1 << 20, bytes_accessed=2 << 20, transcendentals=0),
    )(wanted, parts)


def attend_kernel(
    owners_ref,
    counts_ref,
    arrived_ref,
    query_ref,
    grad_ref,
    self_ref,
    query_out,
    self_out,
    outgoing_ref,
    key_rows,
    value_rows,
    key_grads,
    value_grads,
):
    question = pl.program_id(0)
    live = counts_ref[question]

    @pl.when(question == 0)
    def _():
        outgoing_ref[...] = jnp.zeros_like(outgoing_ref)

    for k in range(CAP):
        owner = owners_ref[question * CAP + k]
        rows = pl.ds(k * MROWS, MROWS)
        key_rows[rows, :] = arrived_ref[owner, :, :HEAD]
        value_rows[rows, :] = arrived_ref[owner, :, HEAD:]
    key_rows[MEM:, :] = self_ref[:, :HEAD]
    value_rows[MEM:, :] = self_ref[:, HEAD:]
    key_block = key_rows[...]
    value_block = value_rows[...]
    key_turned = key_block.T
    pair = 2 * QLEN
    key_index = lax.broadcasted_iota(jnp.int32, (MEM, pair), 0)
    self_index = lax.broadcasted_iota(jnp.int32, (QLEN, pair), 0)
    token = lax.broadcasted_iota(jnp.int32, (QLEN, pair), 1) % QLEN
    allowed = jnp.concatenate([key_index < live * MROWS, self_index <= token], axis=0)
    for g in range(0, GROUP, 2):
        first = slice(g * HEAD, (g + 1) * HEAD)
        second = slice((g + 1) * HEAD, (g + 2) * HEAD)
        queries = jnp.concatenate([query_ref[:, first], query_ref[:, second]], axis=0)
        grads = jnp.concatenate([grad_ref[:, first], grad_ref[:, second]], axis=0)
        scores = jnp.where(allowed, dot(key_block, queries, NT), -1e30)
        top = jnp.max(scores, axis=0, keepdims=True)
        exponent = jnp.exp2((scores - top) * (SCALE * LOG2E))
        probs = exponent * (1.0 / jnp.sum(exponent, axis=0, keepdims=True))
        rounded = probs.astype(jnp.bfloat16)
        prob_grads = dot(value_block, grads, NT)
        delta = jnp.sum(rounded.astype(jnp.float32) * prob_grads, axis=0, keepdims=True)
        score_grads = (probs * (prob_grads - delta) * SCALE).astype(jnp.bfloat16)
        value_part = dot(rounded, grads)
        key_part = dot(score_grads, queries)
        if g == 0:
            value_grads[...] = value_part
            key_grads[...] = key_part
        else:
            value_grads[...] += value_part
            key_grads[...] += key_part
        query_part = dot(key_turned, score_grads)
        query_out[:, first] = query_part[:, :QLEN].T
        query_out[:, second] = query_part[:, QLEN:].T
    self_out[:, :HEAD] = key_grads[MEM:, :]
    self_out[:, HEAD:] = value_grads[MEM:, :]
    for k in range(CAP):
        owner = owners_ref[question * CAP + k]
        rows = pl.ds(k * MROWS, MROWS)

        @pl.when(k < live)
        def _():
            outgoing_ref[owner, :, :HEAD] = key_grads[rows, :].astype(jnp.bfloat16)
            outgoing_ref[owner, :, HEAD:] = value_grads[rows, :].astype(jnp.bfloat16)


def attend(owners, counts, arrived, queries, grads, self_rows):
    token_total, width = queries.shape
    row_width = self_rows.shape[1]
    questions = token_total // QLEN

    def per_question(columns):
        return pl.BlockSpec((QLEN, columns), lambda q, *_: (q, 0))

    return pl.pallas_call(
        attend_kernel,
        grid_spec=pltpu.PrefetchScalarGridSpec(
            num_scalar_prefetch=2,
            grid=(questions,),
            in_specs=[
                whole(arrived.shape),
                per_question(width),
                per_question(width),
                per_question(row_width),
            ],
            out_specs=[per_question(width), per_question(row_width), whole(arrived.shape)],
            scratch_shapes=[
                pltpu.VMEM((KEYS, HEAD), jnp.bfloat16),
                pltpu.VMEM((KEYS, HEAD), jnp.bfloat16),
                pltpu.VMEM((KEYS, HEAD), jnp.float32),
                pltpu.VMEM((KEYS, HEAD), jnp.float32),
            ],
        ),
        out_shape=[
            jax.ShapeDtypeStruct((token_total, width), jnp.float32),
            jax.ShapeDtypeStruct((token_total, row_width), jnp.float32),
            jax.ShapeDtypeStruct(arrived.shape, jnp.bfloat16),
        ],
        compiler_params=params(),
        cost_estimate=pl.CostEstimate(
            flops=2 << 30, bytes_accessed=5 << 20, transcendentals=questions * GROUP * QLEN * KEYS
        ),
    )(owners, counts, arrived, queries, grads, self_rows)


def collect_kernel(wanted_ref, returned_ref, keyvals_ref, out_ref, sums):
    sums[...] = jnp.zeros_like(sums)
    for slot in range(N_WIDE):
        row = wanted_ref[slot]
        place = jnp.where(row < 0, P_DEV, row)
        sums[place] += returned_ref[slot].astype(jnp.float32)
    total = P_DEV * MROWS
    rounded = sums[:P_DEV].reshape(total, 2 * HEAD).astype(jnp.bfloat16)
    out_ref[:total, :] = rounded
    products = rounded.astype(jnp.float32) * keyvals_ref[...].reshape(total, 2 * HEAD)
    inner = lax.dot_general(
        jnp.ones((8, 2 * HEAD), jnp.float32),
        products,
        NT,
        precision=lax.Precision.HIGHEST,
        preferred_element_type=jnp.float32,
    )
    high = inner.astype(jnp.bfloat16)
    low = (inner - high.astype(jnp.float32)).astype(jnp.bfloat16)
    out_ref[total:, :] = jnp.concatenate([high, low], axis=0)


def collect(wanted, returned, keyvals):
    out = (P_DEV * MROWS + 16, 2 * HEAD)
    return pl.pallas_call(
        collect_kernel,
        grid_spec=pltpu.PrefetchScalarGridSpec(
            num_scalar_prefetch=1,
            grid=(1,),
            in_specs=[whole(returned.shape), whole(keyvals.shape)],
            out_specs=whole(out),
            scratch_shapes=[pltpu.VMEM((P_DEV + 1, MROWS, 2 * HEAD), jnp.float32)],
        ),
        out_shape=jax.ShapeDtypeStruct(out, jnp.bfloat16),
        compiler_params=params(),
        cost_estimate=pl.CostEstimate(flops=1 << 20, bytes_accessed=2 << 20, transcendentals=0),
    )(wanted, returned, keyvals)


def finish_kernel(
    all_heads_ref, weight_ref, states_ref, gain_ref, inverse_ref, out_ref, gain_out, mean_ref
):
    heads = all_heads_ref.shape[0]
    total = states_ref.shape[0]

    @pl.when(pl.program_id(0) == 0)
    def _():
        extra = jnp.concatenate([all_heads_ref[h, total:, :] for h in range(heads)], axis=0)
        share = jnp.full((extra.shape[0], HEAD), 1.0 / (8 * D), jnp.bfloat16)
        mean_ref[...] = dot(extra, share, TN)

    weight = weight_ref[0]
    row_grads = dot(all_heads_ref[0, :total, :], weight[: 2 * HEAD, :])
    for h in range(1, heads):
        row_grads += dot(
            all_heads_ref[h, :total, :], weight[h * 2 * HEAD : (h + 1) * 2 * HEAD, :]
        )
    inverse = inverse_ref[:, :1]
    normed = states_ref[...].astype(jnp.float32) * inverse
    gain_out[...] = jnp.sum(row_grads * normed, axis=0, keepdims=True)
    out_ref[...] = (
        inverse * (row_grads * gain_ref[...] - normed * mean_ref[:, :1])
    ).astype(jnp.bfloat16)


def finish(all_heads, weights, states, gain, inverse):
    row_total, features = states.shape
    columns = weights.shape[1]
    halves = weights.shape[0]
    block = 256
    per_half = features // halves // block
    return pl.pallas_call(
        finish_kernel,
        grid=(features // block,),
        in_specs=[
            whole(all_heads.shape),
            pl.BlockSpec((1, columns, block), lambda b: (b // per_half, 0, b % per_half)),
            pl.BlockSpec((row_total, block), lambda b: (0, b)),
            pl.BlockSpec((1, block), lambda b: (0, b)),
            whole(inverse.shape),
        ],
        out_specs=[
            pl.BlockSpec((row_total, block), lambda b: (0, b)),
            pl.BlockSpec((1, block), lambda b: (0, b)),
        ],
        out_shape=[
            jax.ShapeDtypeStruct((row_total, features), jnp.bfloat16),
            jax.ShapeDtypeStruct((1, features), jnp.float32),
        ],
        scratch_shapes=[pltpu.VMEM((row_total, HEAD), jnp.float32)],
        compiler_params=params(),
        cost_estimate=pl.CostEstimate(
            flops=2 * row_total * features * columns, bytes_accessed=7 << 20, transcendentals=0
        ),
    )(all_heads, weights, states, gain, inverse)


def spread(array, axis):
    count = lax.axis_size(axis)
    copies = jnp.broadcast_to(array[None], (count,) + array.shape)
    return lax.all_to_all(copies, axis, 0, 0, tiled=True)


SWAP = ((0, 1), (1, 0))


def on_device(
    passage_states,
    norm_gain,
    proj_weight,
    query_states,
    self_keyvals,
    output_grads,
    passage_ids,
    passage_counts,
):
    wide = ("z", "y", "c")
    core = lax.axis_index("c")
    me = lax.axis_index(wide)
    half = passage_states.shape[1] // 2

    live = jnp.arange(CAP, dtype=jnp.int32)[None, :] < passage_counts[:, None]
    owners = jnp.where(live, passage_ids // P_DEV, 0).reshape(-1)
    places = jnp.where(live, passage_ids % P_DEV + 1, 0).reshape(-1)
    hits = owners[:, None] == jnp.arange(N_WIDE)[None, :]
    requests = jnp.sum(jnp.where(hits, places[:, None], 0), 0).astype(jnp.bfloat16)

    turned = proj_weight.T
    columns = turned.shape[0]
    halves = jnp.transpose(turned.reshape(columns, 2, half), (1, 0, 2))
    ridden = jnp.broadcast_to(requests[None, None], (2, columns, N_WIDE))
    blob = jnp.concatenate([halves, ridden], axis=2)
    blob = lax.all_to_all(blob, "c", 0, 0, tiled=True).reshape(2 * columns, half + N_WIDE)
    blob = spread(blob, "y").reshape(-1, half + N_WIDE)
    blob, passage_states = lax.optimization_barrier((blob, passage_states))
    blob = lax.all_gather(blob, "z", axis=0, tiled=True)

    states = passage_states.astype(jnp.float32)
    squares = lax.psum(jnp.sum(states * states, 1), "mp")
    inverse_rms = lax.rsqrt(squares / D + EPSILON)[:, None]
    memory_rows = (states * inverse_rms * norm_gain).astype(jnp.bfloat16)
    own_rows = lax.dynamic_slice_in_dim(memory_rows, core * half, half, 1)
    give_rows = lax.dynamic_slice_in_dim(memory_rows, (1 - core) * half, half, 1)
    got_rows = lax.ppermute(give_rows, "c", SWAP)

    wanted = blob.reshape(N_WIDE, columns, -1)[:, 0, half:].astype(jnp.int32)
    wanted = jnp.sum(jnp.where(jnp.arange(N_WIDE)[None, :] == me, wanted, 0), 1) - 1

    give_sums = project(got_rows, blob, jnp.bfloat16)
    got_sums = lax.ppermute(give_sums, "c", SWAP)
    own_sums = project(own_rows, blob, jnp.float32)
    partial_sums = (own_sums + got_sums.astype(jnp.float32)).astype(jnp.bfloat16)
    parts = lax.all_to_all(partial_sums, "mp", 0, 0, tiled=True)
    outgoing, keyvals = pack(wanted, parts)
    arrived = lax.all_to_all(outgoing, wide, 0, 0, tiled=True)
    weights = lax.all_gather(blob, "c", axis=0, tiled=False)

    query_gradient, self_keyval_grads, memory_grads = attend(
        owners, passage_counts, arrived, query_states, output_grads, self_keyvals
    )
    returned = lax.all_to_all(memory_grads, wide, 0, 0, tiled=True)
    passage_grads = collect(wanted, returned, keyvals)
    all_heads = spread(passage_grads, "mp").reshape((-1,) + passage_grads.shape)
    inverse_wide = jnp.broadcast_to(inverse_rms, (inverse_rms.shape[0], HEAD))
    state_grads, gain_part = finish(
        all_heads, weights, passage_states, norm_gain[None, :], inverse_wide
    )
    gain_part = lax.psum(gain_part.reshape(-1, HEAD), "c")
    gain_part = jnp.sum(spread(gain_part, "y").reshape(8, -1, HEAD), 0)
    gain_grads = jnp.sum(spread(gain_part, "z").reshape(8, -1), 0)
    return (state_grads, gain_grads, query_gradient, self_keyval_grads)


def solution(mesh):
    grid = Mesh(mesh.devices.reshape(8, 8, 2, 4), ("z", "y", "c", "mp"))
    wide = ("z", "y", "c")
    in_specs = (
        P(wide, "mp"),
        P("mp"),
        P("mp", wide),
        P(wide, "mp"),
        P(wide, "mp"),
        P(wide, "mp"),
        P(wide, None),
        P(wide),
    )
    out_specs = (P(wide, "mp"), P("mp"), P(wide, "mp"), P(wide, "mp"))
    return jax.shard_map(
        on_device, mesh=grid, in_specs=in_specs, out_specs=out_specs, check_vma=False
    )
```

time: 545 us -> 254 us (0.47)
  blocking collectives: 326 us -> 96.1 us
  waiting for transfers between devices: 117 us -> 78.4 us
  Pallas kernels: 0 us -> 24.5 us
  matrix products: 23.4 us -> 0 us
  local copies, waits for them, and re-layouts: 25 us -> 9.35 us
  other arithmetic: 12.6 us -> 5.11 us
    psum x2 -> x1, blocking collectives: 262 us -> 2.46 us  [on_device(): gain_part = lax.psum(gain_part.reshape(-1, HEAD), 'c')]
    all_gather x1 -> x2, waiting for transfers between devices: 77.4 us -> 28.5 us  [the longest x1 28.5 us: on_device(): blob = lax.all_gather(blob, 'z', axis=0, tiled=True)]
    all_to_all x1 -> x5, blocking collectives: 37.2 us -> 83.6 us  [the longest x3 42.7 us: spread(): return lax.all_to_all(copies, axis, 0, 0, tiled=True)]
    pallas_call x0 -> x6, Pallas kernels: none -> 24.5 us  [the longest x1 8.88 us: attend(): pl.pallas_call(attend_kernel, grid_spec=pltpu.PrefetchScalarGridSpec(num_...]
    dot_general x16 -> x0, matrix products: 19.6 us -> none  [the longest x1 4.79 us: on_device(): jnp.dot(memory_rows, whole_weight, preferred_element_type=jnp.float32)]
    all_gather x1 -> x0, blocking collectives: 12.8 us -> none  [on_device(): all_heads = lax.all_gather(passage_grads, 'mp', axis=1, tiled=True)]
    all_to_all x2 -> x3, waiting for transfers between devices: 39.3 us -> 47.3 us  [the longest x1 29.5 us: on_device(): arrived = lax.all_to_all(outgoing, wide, 0, 0, tiled=True)]
    all_to_all x2 -> x3, starting transfers between devices: 23.4 us -> 21.1 us  [the longest x1 11.4 us: on_device(): arrived = lax.all_to_all(outgoing, wide, 0, 0, tiled=True)]
  transfers between devices with their start and end apart: 4 -> 7, of which waited for: 3 -> 5; matrix products, arithmetic and copies ran while one was open for 1% -> 1% of each run, Pallas kernels for 0% -> 5%
where the time goes in v1:
time: 254 us; the launch traced here: 253 us
  blocking collectives  96.1 us (38%)
  waiting for transfers between devices  78.4 us (31%)
  starting transfers between devices  25 us (10%)
  Pallas kernels  24.5 us (10%)
  between operations  14.2 us (6%)
  local copies, waits for them, and re-layouts  9.35 us (4%)
  other arithmetic  5.11 us (2%)
    all_to_all x3, blocking collectives, spread(): return lax.all_to_all(copies, axis, 0, 0, tiled=True)  42.7 us
    all_to_all x1, blocking collectives, on_device(): returned = lax.all_to_all(memory_grads, wide, 0, 0, tiled=True)  37.2 us
    all_to_all x1, waiting for transfers between devices, on_device(): arrived = lax.all_to_all(outgoing, wide, 0, 0, tiled=True)  29.5 us
    all_gather x1, waiting for transfers between devices, on_device(): blob = lax.all_gather(blob, 'z', axis=0, tiled=True)  28.5 us
    all_to_all x1, starting transfers between devices, on_device(): arrived = lax.all_to_all(outgoing, wide, 0, 0, tiled=True)  11.4 us
    psum x1, blocking collectives, on_device(): squares = lax.psum(jnp.sum(states * states, 1), 'mp')  10 us
    all_to_all x1, waiting for transfers between devices, spread(): return lax.all_to_all(copies, axis, 0, 0, tiled=True)  9.04 us
    pallas_call x1, Pallas kernels, attend(): pl.pallas_call(attend_kernel, grid_spec=pltpu.PrefetchScalarGridSpec(num_...  8.88 us
  transfers between devices with their start and end apart: 7, of which 5 were waited for; matrix products, arithmetic and copies ran while one was open for 1% of the time, Pallas kernels for 5%

profile of v1, /device:TPU:2, one launch (start us, length us, event | category | flops | bytes accessed | tf_op | source)
XLA Modules:
  0.0 252.7 jit_solution(1760451373969233660)
XLA Ops:
  9.1 3.7 %all_to_all.40 = bf16[2,8,1152]{2,1,0:T(8,128)(2,1)S(1)} all-to-all(bf16[2,8,1152]{2,1,0:T(8,128)(2,1)S(1)} %pad_maximum_fusion), channel_id=1, replica_groups=mesh['z'=8,'y'=8,'c'=2,'mp'=4] {'c'}, dimensions={0} | all-to-all | bytes 73728 | tf_op jit(solution)/shard_map/all_to_all | solution.py:341
  12.9 19.9 %all_to_all.41 = bf16[8,16,1152]{2,1,0:T(8,128)(2,1)} all-to-all(bf16[8,16,1152]{2,1,0:T(8,128)(2,1)S(1)} %broadcast_in_dim.80), channel_id=1, replica_groups=mesh['z'=8,'y'=8,'c'=2,'mp'=4] {'y'}, dimensions={0} | all-to-all | bytes 589824 | tf_op jit(solution)/shard_map/all_to_all | solution.py:309
  33.1 10.0 %psum.14 = f32[256]{0:T(256)S(1)} all-reduce(f32[256]{0:T(256)S(1)} %fusion), channel_id=1, replica_groups=mesh['z'=8,'y'=8,'c'=2,'mp'=4] {'mp'}, use_global_device_ids=true, to_apply=%region_3.4 | all-reduce | flops 256 | bytes 2048 | tf_op jit(solution)/shard_map/psum | solution.py:347
  44.4 1.9 collective-permute-start
  46.3 1.9 collective-permute-done.rows_ref
  49.0 28.5 %all-gather.4.cloned.1.call-done.weight_ref = bf16[1024,1152]{1,0:T(8,128)(2,1)} async-done(((bf16[128,1152]{1,0:T(8,128)(2,1)}), bf16[1024,1152]{1,0:T(8,128)(2,1)}) %all-gather.4.cloned.1.call-update) | async-done | bytes 2359312 | tf_op jit(solution)/shard_map/all_gather | solution.py:344
  77.5 1.7 copy-done
  80.2 2.5 shard_map.112
  82.7 1.9 collective-permute-start.1
  87.2 2.0 add_convert_fusion
  89.2 4.8 %all-to-all-start.2 = ((bf16[4,256,256]{2,1,0:T(8,128)(2,1)}), bf16[4,256,256]{2,1,0:T(8,128)(2,1)}, u32[]{:S(2)}, u32[]{:S(2)}) async-start(bf16[4,256,256]{2,1,0:T(8,128)(2,1)} %add_convert_fusion), calls=%async_computation.2 | async-start | bytes 1048576 | tf_op jit(solution)/shard_map/all_to_all | solution.py:361
  94.2 8.7 %all-to-all-done.2.parts_ref = bf16[4,256,256]{2,1,0:T(8,128)(2,1)} async-done(((bf16[4,256,256]{2,1,0:T(8,128)(2,1)}), bf16[4,256,256]{2,1,0:T(8,128)(2,1)}, u32[]{:S(2)}, u32[]{:S(2)}) %all-to-all-start.2) | async-done | bytes 524320 | tf_op jit(solution)/shard_map/all_to_all | solution.py:361
  102.9 2.8 %shard_map.113 = (bf16[128,16,256]{2,1,0:T(8,128)(2,1)}, f32[16,16,256]{2,1,0:T(8,128)S(1)}) custom-call(s32[128]{0:T(128)S(1)} %broadcast_add_fusion.wanted_ref, bf16[4,256,256]{2,1,0:T(8,128)(2,1)} %all-to-all-done.2.parts_ref), custom_call_target="tpu_custom_call" | custom-call | flops 1048576 | bytes 2097152 | tf_op jit(solution)/shard_map/pallas_call | solution.py:79
  105.7 11.4 %all-to-all-start.3 = ((bf16[128,16,256]{2,1,0:T(8,128)(2,1)}), bf16[128,16,256]{2,1,0:T(8,128)(2,1)S(1)}, u32[]{:S(2)}, u32[]{:S(2)}) async-start(bf16[128,16,256]{2,1,0:T(8,128)(2,1)} %get-tuple-element.15), calls=%async_computation.3 | async-start | bytes 2097152 | tf_op jit(solution)/shard_map/all_to_all | solution.py:363
  117.9 29.5 %all-to-all-done.3.arrived_ref = bf16[128,16,256]{2,1,0:T(8,128)(2,1)S(1)} async-done(((bf16[128,16,256]{2,1,0:T(8,128)(2,1)}), bf16[128,16,256]{2,1,0:T(8,128)(2,1)S(1)}, u32[]{:S(2)}, u32[]{:S(2)}) %all-to-all-start.3) | async-done | bytes 1048608 | tf_op jit(solution)/shard_map/all_to_all | solution.py:363
  150.2 8.9 %shard_map.114 = (f32[256,1024]{1,0:T(8,128)}, f32[256,256]{1,0:T(8,128)}, bf16[128,16,256]{2,1,0:T(8,128)(2,1)S(1)}) custom-call(s32[64]{0:T(128)S(1)} %copy-done.12, s32[2]{0:T(128)S(1)} %copy-done.7, bf16[128,16,256]{2,1,0:T(8,128)(2,1)S(1)} %all-to-all-done.3.arrived_ref, bf16[256,1024]{1,0:T(8,128)(2,1)S(1)} %copy-done.8, ...), custom_call_target="tpu_custom_call" | custom-call | flops 2147483648 | bytes 5242880 | tf_op jit(solution)/shard_map/pallas_call | solution.py:178
  159.0 37.2 %all_to_all.42.returned_ref = bf16[128,16,256]{2,1,0:T(8,128)(2,1)S(1)} all-to-all(bf16[128,16,256]{2,1,0:T(8,128)(2,1)S(1)} %get-tuple-element.16), channel_id=1, replica_groups=mesh['z'=8,'y'=8,'c'=2,'mp'=4] {'z','y','c'}, dimensions={0} | all-to-all | bytes 2097152 | tf_op jit(solution)/shard_map/all_to_all | solution.py:369
  196.2 1.6 shard_map.115
  198.7 4.9 %all-to-all-start.5 = ((bf16[4,272,256]{2,1,0:T(8,128)(2,1)}), bf16[4,272,256]{2,1,0:T(8,128)(2,1)S(1)}, u32[]{:S(2)}, u32[]{:S(2)}) async-start(bf16[4,272,256]{2,1,0:T(8,128)(2,1)} %broadcast_in_dim.82), calls=%async_computation.5 | async-start | bytes 1114112 | tf_op jit(solution)/shard_map/all_to_all | solution.py:309
  203.6 9.0 %all-to-all-done.5.all_heads_ref = bf16[4,272,256]{2,1,0:T(8,128)(2,1)S(1)} async-done(((bf16[4,272,256]{2,1,0:T(8,128)(2,1)}), bf16[4,272,256]{2,1,0:T(8,128)(2,1)S(1)}, u32[]{:S(2)}, u32[]{:S(2)}) %all-to-all-start.5) | async-done | bytes 557088 | tf_op jit(solution)/shard_map/all_to_all | solution.py:309
  212.7 7.2 %shard_map.116 = (bf16[256,2048]{1,0:T(8,128)(2,1)}, f32[1,2048]{1,0:T(1,128)S(1)}) custom-call(bf16[4,272,256]{2,1,0:T(8,128)(2,1)S(1)} %all-to-all-done.5.all_heads_ref, bf16[2,1024,1152]{2,1,0:T(8,128)(2,1)} %bitcast.16, bf16[256,2048]{1,0:T(8,128)(2,1)S(1)} %copy-done.2, f32[1,2048]{1,0:T(1,128)S(1)} %bitcast.14, f32[256,128]{1,0:T(8,128)S(1)} %broadcast_in_dim.84.inverse_ref), custom_call_target="tpu_custom_call" | custom-call | flops 1073741824 | bytes 7340032 | tf_op jit(solution)/shard_map/pallas_call | solution.py:280
  219.9 2.5 psum.15
  222.4 12.0 %all_to_all.43 = f32[8,16,128]{2,1,0:T(8,128)S(1)} all-to-all(f32[8,16,128]{2,1,0:T(8,128)S(1)} %broadcast_in_dim.85), channel_id=1, replica_groups=mesh['z'=8,'y'=8,'c'=2,'mp'=4] {'y'}, dimensions={0} | all-to-all | bytes 131072 | tf_op jit(solution)/shard_map/all_to_all | solution.py:309
  234.5 10.8 %all_to_all.44 = f32[8,16,128]{2,1,0:T(8,128)S(1)} all-to-all(f32[8,16,128]{2,1,0:T(8,128)S(1)} %broadcast_in_dim.86), channel_id=1, replica_groups=mesh['z'=8,'y'=8,'c'=2,'mp'=4] {'z'}, dimensions={0} | all-to-all | bytes 131072 | tf_op jit(solution)/shard_map/all_to_all | solution.py:309
  (54 shorter events, 13.1 us)
Async XLA Ops:
  7.2 25.7 %copy-start.2 = (bf16[256,2048]{1,0:T(8,128)(2,1)S(1)}, bf16[256,2048]{1,0:T(8,128)(2,1)}, u32[]{:S(2)}) copy-start(bf16[256,2048]{1,0:T(8,128)(2,1)} %states_ref) | copy-start | bytes 3145732
  7.2 36.0 %copy-start.6 = (f32[2048]{0:T(1024)S(1)}, f32[2048]{0:T(1024)}, u32[]{:S(2)}) copy-start(f32[2048]{0:T(1024)} %param.9) | copy-start | bytes 24580
  7.2 70.3 %all-gather.4.cloned.1.call-start = ((), (), s32[]{:S(2)}) async-start(), calls=%async_computation.8 | async-start | bytes 2654208 | tf_op jit(solution)/shard_map/all_gather | solution.py:344
  8.2 35.2 %copy-start.11 = (s32[64]{0:T(128)}, s32[64]{0:T(128)S(1)}, u32[]{:S(2)}) copy-start(s32[64]{0:T(128)S(1)} %eq.30.owners_ref) | copy-start | bytes 772
  44.4 3.8 %collective-permute-start = (bf16[256,1024]{1,0:T(8,128)(2,1)S(1)}, bf16[256,1024]{1,0:T(8,128)(2,1)S(1)}, u32[]{:S(2)}, u32[]{:S(2)}) collective-permute-start(bf16[256,1024]{1,0:T(8,128)(2,1)S(1)} %get-tuple-element.22), channel_id=1, source_target_pairs={{0,4},{4,0},{1,5},{5,1},{2,6},{6,2},{3,7},{7,3},{8,12},{12,8},{9,1... | collective-permute-start | bytes 1572872 | tf_op jit(solution)/shard_map/ppermute | solution.py:352
  48.2 0.8 copy-start.4
  77.5 1.7 copy-start
  79.1 1.0 copy-start.5
  80.2 4.4 %copy-start.1 = (bf16[1024,1152]{1,0:T(8,128)(2,1)S(1)}, bf16[1024,1152]{1,0:T(8,128)(2,1)}, u32[]{:S(2)}) copy-start(bf16[1024,1152]{1,0:T(8,128)(2,1)} %all-gather.4.cloned.1.call-done.weight_ref) | copy-start | bytes 7077892
  82.7 4.5 %collective-permute-start.1 = (bf16[4,256,256]{2,1,0:T(8,128)(2,1)}, bf16[4,256,256]{2,1,0:T(8,128)(2,1)}, u32[]{:S(2)}, u32[]{:S(2)}) collective-permute-start(bf16[4,256,256]{2,1,0:T(8,128)(2,1)} %shard_map.112), channel_id=1, source_target_pairs={{0,4},{4,0},{1,5},{5,1},{2,6},{6,2},{3,7},{7,3},{8,12},{12,8},{9,1... | collective-permute-start | bytes 1572872 | tf_op jit(solution)/shard_map/ppermute | solution.py:358
  84.6 1.0 copy-start.3
  89.2 13.7 %all-to-all-start.2 = ((bf16[4,256,256]{2,1,0:T(8,128)(2,1)}), bf16[4,256,256]{2,1,0:T(8,128)(2,1)}, u32[]{:S(2)}, u32[]{:S(2)}) async-start(bf16[4,256,256]{2,1,0:T(8,128)(2,1)} %add_convert_fusion), calls=%async_computation.2 | async-start | bytes 1048576 | tf_op jit(solution)/shard_map/all_to_all | solution.py:361
  105.7 41.7 %copy-start.7 = (s32[2]{0:T(128)S(1)}, s32[2]{0:T(128)}, u32[]{:S(2)}) copy-start(s32[2]{0:T(128)} %counts_ref.1) | copy-start | bytes 28
  105.7 41.7 %copy-start.10 = (bf16[256,256]{1,0:T(8,128)(2,1)S(1)}, bf16[256,256]{1,0:T(8,128)(2,1)}, u32[]{:S(2)}) copy-start(bf16[256,256]{1,0:T(8,128)(2,1)} %self_ref.1) | copy-start | bytes 393220
  105.7 41.7 %all-to-all-start.3 = ((bf16[128,16,256]{2,1,0:T(8,128)(2,1)}), bf16[128,16,256]{2,1,0:T(8,128)(2,1)S(1)}, u32[]{:S(2)}, u32[]{:S(2)}) async-start(bf16[128,16,256]{2,1,0:T(8,128)(2,1)} %get-tuple-element.15), calls=%async_computation.3 | async-start | bytes 2097152 | tf_op jit(solution)/shard_map/all_to_all | solution.py:363
  117.1 86.5 %all-gather.6.cloned.1.call-start = ((), (), s32[]{:S(2)}) async-start(), calls=%async_computation.9 | async-start | bytes 7077888 | tf_op jit(solution)/shard_map/all_gather | solution.py:364
  147.4 1.0 copy-start.8
  148.5 1.0 copy-start.9
  149.5 0.7 copy-start.12
  198.7 13.9 %all-to-all-start.5 = ((bf16[4,272,256]{2,1,0:T(8,128)(2,1)}), bf16[4,272,256]{2,1,0:T(8,128)(2,1)S(1)}, u32[]{:S(2)}, u32[]{:S(2)}) async-start(bf16[4,272,256]{2,1,0:T(8,128)(2,1)} %broadcast_in_dim.82), calls=%async_computation.5 | async-start | bytes 1114112 | tf_op jit(solution)/shard_map/all_to_all | solution.py:309
Sparse Core Ops, SparseCore 0:
  32.9 44.4 all-gather.3
  120.1 22.1 all-gather.5

commit v2 on v0

v2 whole, which is shorter than its diff:
```python
import math

import jax
import jax.numpy as jnp
from jax import lax
from jax.experimental import pallas as pl
from jax.experimental.pallas import tpu as pltpu
from jax.sharding import Mesh
from jax.sharding import PartitionSpec as P

D = 8192
MROWS = 16
HEAD = 128
GROUP = 8
QLEN = 128
CAP = 32
MEM = CAP * MROWS
KEYS = MEM + QLEN
N_WIDE = 128
P_DEV = 16
EPSILON = 1e-05
SCALE = 1.0 / math.sqrt(HEAD)
LOG2E = math.log2(math.e)
FEW, MANY = 32 * 1024 * 1024, 60 * 1024 * 1024

NT = (((1,), (1,)), ((), ()))
TN = (((0,), (0,)), ((), ()))
SWAP = ((0, 1), (1, 0))
VMEM = pl.BlockSpec(memory_space=pltpu.VMEM)
SMEM = pl.BlockSpec(memory_space=pltpu.SMEM)
HBM = pl.BlockSpec(memory_space=pltpu.HBM)


def dot(a, b, dims=(((1,), (0,)), ((), ()))):
    return lax.dot_general(a, b, dims, preferred_element_type=jnp.float32)


def kernel_call(
    body, scalars, arrays, out_shapes, scratch=(), flops=1 << 20, moved=2 << 20, given=VMEM, out=VMEM, limit=MANY
):
    return pl.pallas_call(
        body,
        in_specs=[SMEM] * len(scalars) + [given] * len(arrays),
        out_specs=[out] * len(out_shapes),
        out_shape=[jax.ShapeDtypeStruct(*one) for one in out_shapes],
        scratch_shapes=list(scratch),
        compiler_params=pltpu.CompilerParams(vmem_limit_bytes=limit),
        cost_estimate=pl.CostEstimate(flops=flops, bytes_accessed=moved, transcendentals=0),
    )(*scalars, *arrays)


def wide_as(columns, width):
    return jnp.concatenate([columns] * (width // columns.shape[1]), axis=1)


def project_kernel(place_ref, rows_ref, weight_ref, *refs):
    *others, out_ref = refs
    half = rows_ref.shape[1] // 2
    rows = rows_ref[:, pl.ds(pl.multiple_of(place_ref[0] * half, half), half)]
    for h in range(out_ref.shape[0]):
        total = dot(rows, weight_ref[h * 2 * HEAD : (h + 1) * 2 * HEAD, :half], NT)
        for other in others:
            total = total + other[h]
        out_ref[h] = total.astype(out_ref.dtype)


def project(place, rows, weight, dtype, *others):
    shape = (weight.shape[0] // (2 * HEAD), rows.shape[0], 2 * HEAD)
    (sums,) = kernel_call(
        project_kernel,
        (place,),
        (rows, weight) + others,
        [(shape, dtype)],
        flops=1 << 29,
        moved=4 << 20,
        limit=FEW,
    )
    return sums


PACK_STEPS = 4


def pack_kernel(
    wanted_ref,
    parts_ref,
    out_hbm,
    keyvals_hbm,
    out_ref,
    keyvals_ref,
    table_ref,
    sems,
):
    total = parts_ref[0].astype(jnp.float32)
    for part in range(1, parts_ref.shape[0]):
        total = total + parts_ref[part].astype(jnp.float32)
    total = total.reshape(P_DEV, MROWS, 2 * HEAD)
    keyvals_ref[...] = total
    copies = [pltpu.make_async_copy(keyvals_ref, keyvals_hbm, sems.at[PACK_STEPS])]
    copies[0].start()
    table_ref[...] = total.astype(jnp.bfloat16)
    slots = N_WIDE // PACK_STEPS
    for step in range(PACK_STEPS):
        for slot in range(step * slots, (step + 1) * slots):
            out_ref[slot] = table_ref[jnp.maximum(wanted_ref[slot], 0)]
        done = pl.ds(step * slots, slots)
        copies.append(pltpu.make_async_copy(out_ref.at[done], out_hbm.at[done], sems.at[step]))
        copies[-1].start()
    for copy in copies:
        copy.wait()


def attend_kernel(
    slots_ref,
    arrived_hbm,
    query_hbm,
    grad_hbm,
    self_hbm,
    query_out_hbm,
    self_out_hbm,
    outgoing_hbm,
    arrived_ref,
    query_ref,
    grad_ref,
    self_ref,
    query_out,
    self_out,
    outgoing_ref,
    key_rows,
    value_rows,
    key_grads,
    value_grads,
    in_sems,
    out_sems,
    question_sems,
):
    loads = [
        pltpu.make_async_copy(source, target, in_sems.at[index])
        for index, (source, target) in enumerate(
            [
                (arrived_hbm, arrived_ref),
                (query_hbm, query_ref),
                (grad_hbm, grad_ref),
                (self_hbm, self_ref),
            ]
        )
    ]
    for load in loads:
        load.start()
    outgoing_ref[...] = jnp.zeros_like(outgoing_ref)
    for load in loads:
        load.wait()
    pair = 2 * QLEN
    key_index = lax.broadcasted_iota(jnp.int32, (MEM, pair), 0)
    self_index = lax.broadcasted_iota(jnp.int32, (QLEN, pair), 0)
    token = lax.broadcasted_iota(jnp.int32, (QLEN, pair), 1) % QLEN

    @pl.loop(0, query_ref.shape[0] // QLEN)
    def _(question):
        live = slots_ref[SLOTS + question]
        tokens = pl.ds(pl.multiple_of(question * QLEN, QLEN), QLEN)
        for k in range(CAP):
            slot = slots_ref[question * CAP + k]
            key_rows[k * MROWS : (k + 1) * MROWS, :] = arrived_ref[slot, :, :HEAD]
            value_rows[k * MROWS : (k + 1) * MROWS, :] = arrived_ref[slot, :, HEAD:]
        key_rows[MEM:, :] = self_ref[tokens, :HEAD]
        value_rows[MEM:, :] = self_ref[tokens, HEAD:]
        key_block = key_rows[...]
        value_block = value_rows[...]
        key_turned = key_block.T
        allowed = jnp.concatenate([key_index < live * MROWS, self_index <= token], axis=0)
        for g in range(0, GROUP, 2):
            first = slice(g * HEAD, (g + 1) * HEAD)
            second = slice((g + 1) * HEAD, (g + 2) * HEAD)
            queries = jnp.concatenate([query_ref[tokens, first], query_ref[tokens, second]], axis=0)
            grads = jnp.concatenate([grad_ref[tokens, first], grad_ref[tokens, second]], axis=0)
            scores = jnp.where(allowed, dot(key_block, queries, NT), -1e30)
            top = jnp.max(scores, axis=0, keepdims=True)
            exponent = jnp.exp2((scores - top) * (SCALE * LOG2E))
            probs = exponent * (1.0 / jnp.sum(exponent, axis=0, keepdims=True))
            rounded = probs.astype(jnp.bfloat16)
            prob_grads = dot(value_block, grads, NT)
            delta = jnp.sum(rounded.astype(jnp.float32) * prob_grads, axis=0, keepdims=True)
            score_grads = (probs * (prob_grads - delta) * SCALE).astype(jnp.bfloat16)
            value_part = dot(rounded, grads)
            key_part = dot(score_grads, queries)
            if g == 0:
                value_grads[...] = value_part
                key_grads[...] = key_part
            else:
                value_grads[...] += value_part
                key_grads[...] += key_part
            query_part = dot(key_turned, score_grads)
            query_out[tokens, first] = query_part[:, :QLEN].T
            query_out[tokens, second] = query_part[:, QLEN:].T
        pltpu.make_async_copy(
            query_out.at[tokens], query_out_hbm.at[tokens], question_sems.at[question]
        ).start()
        self_out[tokens, :HEAD] = key_grads[MEM:, :]
        self_out[tokens, HEAD:] = value_grads[MEM:, :]
        for k in range(CAP):
            slot = slots_ref[question * CAP + k]
            rows = slice(k * MROWS, (k + 1) * MROWS)

            @pl.when(k < live)
            def _():
                outgoing_ref[slot, :, :HEAD] = key_grads[rows, :].astype(jnp.bfloat16)
                outgoing_ref[slot, :, HEAD:] = value_grads[rows, :].astype(jnp.bfloat16)

    stores = [
        pltpu.make_async_copy(outgoing_ref, outgoing_hbm, out_sems.at[0]),
        pltpu.make_async_copy(self_out, self_out_hbm, out_sems.at[1]),
    ]
    for store in stores:
        store.start()
    for question in range(query_ref.shape[0] // QLEN):
        tokens = pl.ds(question * QLEN, QLEN)
        stores.append(
            pltpu.make_async_copy(
                query_out.at[tokens], query_out_hbm.at[tokens], question_sems.at[question]
            )
        )
    for store in stores:
        store.wait()


def attend(slots, arrived, queries, grads, self_rows):
    return kernel_call(
        attend_kernel,
        (slots,),
        (arrived, queries, grads, self_rows),
        [
            (queries.shape, jnp.float32),
            (self_rows.shape, jnp.float32),
            (arrived.shape, jnp.bfloat16),
        ],
        [
            pltpu.VMEM(arrived.shape, jnp.bfloat16),
            pltpu.VMEM(queries.shape, jnp.bfloat16),
            pltpu.VMEM(grads.shape, jnp.bfloat16),
            pltpu.VMEM(self_rows.shape, jnp.bfloat16),
            pltpu.VMEM(queries.shape, jnp.float32),
            pltpu.VMEM(self_rows.shape, jnp.float32),
            pltpu.VMEM(arrived.shape, jnp.bfloat16),
        ]
        + [pltpu.VMEM((KEYS, HEAD), jnp.bfloat16)] * 2
        + [pltpu.VMEM((KEYS, HEAD), jnp.float32)] * 2
        + [pltpu.SemaphoreType.DMA((4,)), pltpu.SemaphoreType.DMA((2,)), pltpu.SemaphoreType.DMA((2,))],
        flops=2 << 30,
        moved=5 << 20,
        given=HBM,
        out=HBM,
    )


def collect_kernel(wanted_ref, returned_ref, keyvals_ref, out_ref, sums):
    sums[...] = jnp.zeros_like(sums)
    for slot in range(N_WIDE):
        row = wanted_ref[slot]
        sums[jnp.where(row < 0, P_DEV, row)] += returned_ref[slot].astype(jnp.float32)
    total = P_DEV * MROWS
    rounded = sums[:P_DEV].reshape(total, 2 * HEAD).astype(jnp.bfloat16)
    products = rounded.astype(jnp.float32) * keyvals_ref[...].reshape(total, 2 * HEAD)
    inner = lax.dot_general(
        jnp.ones((8, 2 * HEAD), jnp.float32),
        products,
        NT,
        precision=lax.Precision.HIGHEST,
        preferred_element_type=jnp.float32,
    )
    high = inner.astype(jnp.bfloat16)
    low = (inner - high.astype(jnp.float32)).astype(jnp.bfloat16)
    out_ref[:total, :] = rounded
    out_ref[total:, :] = jnp.concatenate([high, low], axis=0)


BLOCK = 256


def row_blocks(place_ref, all_heads_ref, weight_refs, states_ref, inverse_ref, finish):
    core = place_ref[0]
    total, features = states_ref.shape
    half = features // 2
    inverse = wide_as(inverse_ref[...], BLOCK)
    for place in range(2):
        start = (core if place == 0 else 1 - core) * half
        for block in range(half // BLOCK):
            span = slice(block * BLOCK, (block + 1) * BLOCK)
            row_grads = None
            for h in range(all_heads_ref.shape[0]):
                weight = weight_refs[place][h * 2 * HEAD : (h + 1) * 2 * HEAD, span]
                part = dot(all_heads_ref[h, :total, :], weight)
                row_grads = part if row_grads is None else row_grads + part
            lanes = pl.ds(pl.multiple_of(start + block * BLOCK, BLOCK), BLOCK)
            normed = states_ref[:, lanes].astype(jnp.float32) * inverse
            finish(lanes, row_grads, normed, inverse)


def gain_kernel(place_ref, all_heads_ref, w0, w1, states_ref, inverse_ref, out_ref):
    def finish(lanes, row_grads, normed, inverse):
        out_ref[:, lanes] = jnp.sum(row_grads * normed, axis=0, keepdims=True)

    row_blocks(place_ref, all_heads_ref, (w0, w1), states_ref, inverse_ref, finish)


def state_kernel(place_ref, all_heads_ref, w0, w1, states_ref, inverse_ref, gain_ref, out_ref):
    total = states_ref.shape[0]
    heads = all_heads_ref.shape[0]
    extra = jnp.concatenate([all_heads_ref[h, total:, :] for h in range(heads)], axis=0)
    share = jnp.full((extra.shape[0], HEAD), 1.0 / (8 * D), jnp.bfloat16)
    mean = wide_as(dot(extra, share, TN), BLOCK)

    def finish(lanes, row_grads, normed, inverse):
        scaled = row_grads * gain_ref[:, lanes]
        out_ref[:, lanes] = (inverse * (scaled - normed * mean)).astype(jnp.bfloat16)

    row_blocks(place_ref, all_heads_ref, (w0, w1), states_ref, inverse_ref, finish)


def spread(array, axis):
    count = lax.axis_size(axis)
    copies = jnp.broadcast_to(array[None], (count,) + array.shape)
    return lax.all_to_all(copies, axis, 0, 0, tiled=True)


WIDE = ("z", "y", "c")
SLOTS = 2 * CAP


def on_device(
    passage_states,
    norm_gain,
    proj_weight,
    query_states,
    self_keyvals,
    output_grads,
    passage_ids,
    passage_counts,
):
    core = lax.axis_index("c")
    place = jnp.stack([core, 1 - core]).astype(jnp.int32)
    me = lax.axis_index(WIDE)
    half = passage_states.shape[1] // 2

    live = jnp.arange(CAP, dtype=jnp.int32)[None, :] < passage_counts[:, None]
    owners = jnp.where(live, passage_ids // P_DEV, 0).reshape(-1)
    places = jnp.where(live, passage_ids % P_DEV + 1, 0).reshape(-1)
    hits = owners[:, None] == jnp.arange(N_WIDE)[None, :]
    requests = jnp.sum(jnp.where(hits, places[:, None], 0), 0).astype(jnp.bfloat16)

    turned = proj_weight.T
    columns = turned.shape[0]
    halves = jnp.transpose(turned.reshape(columns, 2, half), (1, 0, 2))
    ridden = jnp.broadcast_to(requests[None, None], (2, columns, N_WIDE))
    blob = jnp.concatenate([halves, ridden], axis=2)
    blob = lax.all_to_all(blob, "c", 0, 0, tiled=True).reshape(2 * columns, half + N_WIDE)
    blob = spread(blob, "y").reshape(-1, half + N_WIDE)
    blob, passage_states = lax.optimization_barrier((blob, passage_states))
    blob = lax.all_gather(blob, "z", axis=0, tiled=True)

    states = passage_states.astype(jnp.float32)
    squares = lax.psum(jnp.sum(states * states, 1), "mp")
    inverse_rms = lax.rsqrt(squares / D + EPSILON)[:, None]
    memory_rows = (states * inverse_rms * norm_gain).astype(jnp.bfloat16)
    inverse = jnp.broadcast_to(inverse_rms, (inverse_rms.shape[0], HEAD))
    weight, memory_rows, inverse = lax.optimization_barrier((blob, memory_rows, inverse))

    other_weight = lax.ppermute(weight, "c", SWAP)
    own_sums = project(place, memory_rows, weight, jnp.float32)
    partial_sums = project(place[::-1], memory_rows, other_weight, jnp.bfloat16, own_sums)
    wanted = weight.reshape(N_WIDE, columns, -1)[:, 0, half:].astype(jnp.int32)
    wanted = jnp.sum(jnp.where(jnp.arange(N_WIDE)[None, :] == me, wanted, 0), 1) - 1
    partial_sums, wanted = lax.optimization_barrier((partial_sums, wanted))
    parts = lax.all_to_all(partial_sums, "mp", 0, 0, tiled=True)
    table = (P_DEV, MROWS, 2 * HEAD)
    outgoing, keyvals = kernel_call(
        pack_kernel,
        (wanted,),
        (parts,),
        [((N_WIDE, MROWS, 2 * HEAD), jnp.bfloat16), (table, jnp.float32)],
        [
            pltpu.VMEM((N_WIDE, MROWS, 2 * HEAD), jnp.bfloat16),
            pltpu.VMEM(table, jnp.float32),
            pltpu.VMEM(table, jnp.bfloat16),
            pltpu.SemaphoreType.DMA((PACK_STEPS + 1,)),
        ],
        out=HBM,
    )
    slots = jnp.concatenate([owners, passage_counts])
    outgoing, slots = lax.optimization_barrier((outgoing, slots))
    arrived = lax.all_to_all(outgoing, WIDE, 0, 0, tiled=True)
    query_gradient, self_keyval_grads, memory_grads = attend(
        slots, arrived, query_states, output_grads, self_keyvals
    )
    returned = lax.all_to_all(memory_grads, WIDE, 0, 0, tiled=True)
    (passage_grads,) = kernel_call(
        collect_kernel,
        (wanted,),
        (returned, keyvals),
        [((P_DEV * MROWS + 16, 2 * HEAD), jnp.bfloat16)],
        [pltpu.VMEM((P_DEV + 1, MROWS, 2 * HEAD), jnp.float32)],
        limit=FEW,
    )
    all_heads = spread(passage_grads, "mp")
    last = (all_heads, weight, other_weight, passage_states, inverse)
    features = passage_states.shape[1]
    (gain_part,) = kernel_call(
        gain_kernel,
        (place,),
        last,
        [((1, features), jnp.float32)],
        flops=1 << 30,
        moved=6 << 20,
        limit=FEW,
    )
    gain_part = lax.psum(gain_part.reshape(-1, HEAD), "c").astype(jnp.bfloat16)
    gain_grads = jnp.sum(spread(gain_part, ("z", "y")).astype(jnp.float32), 0).reshape(-1)
    (state_grads,) = kernel_call(
        state_kernel,
        (place,),
        last + (norm_gain[None, :],),
        [(passage_states.shape, jnp.bfloat16)],
        flops=1 << 30,
        moved=7 << 20,
        limit=FEW,
    )
    return (state_grads, gain_grads, query_gradient, self_keyval_grads)


def solution(mesh):
    grid = Mesh(mesh.devices.reshape(8, 8, 2, 4), WIDE + ("mp",))
    in_specs = (
        P(WIDE, "mp"),
        P("mp"),
        P("mp", WIDE),
        P(WIDE, "mp"),
        P(WIDE, "mp"),
        P(WIDE, "mp"),
        P(WIDE, None),
        P(WIDE),
    )
    out_specs = (P(WIDE, "mp"), P("mp"), P(WIDE, "mp"), P(WIDE, "mp"))
    return jax.shard_map(
        on_device, mesh=grid, in_specs=in_specs, out_specs=out_specs, check_vma=False
    )
```

time: 545 us -> 245 us (0.45)
  the two profiles are of different devices: /device:TPU:2 before, /device:TPU:8 now
where the time goes in v2:
time: 245 us; the launch traced here: 244 us
  blocking collectives  128 us (52%)
  waiting for transfers between devices  50.7 us (21%)
  Pallas kernels  21.6 us (9%)
  between operations  14.3 us (6%)
  starting transfers between devices  12 us (5%)
  local copies, waits for them, and re-layouts  10.1 us (4%)
  other arithmetic  6.96 us (3%)
    all_to_all x1, blocking collectives, on_device(): arrived = lax.all_to_all(outgoing, WIDE, 0, 0, tiled=True)  42.5 us
    all_to_all x1, blocking collectives, on_device(): returned = lax.all_to_all(memory_grads, WIDE, 0, 0, tiled=True)  37.5 us
    all_gather x1, waiting for transfers between devices, on_device(): blob = lax.all_gather(blob, 'z', axis=0, tiled=True)  33.5 us
    all_to_all x2, blocking collectives, spread(): return lax.all_to_all(copies, axis, 0, 0, tiled=True)  32.7 us
    pallas_call x7, Pallas kernels, kernel_call(): pl.pallas_call(body, in_specs=[SMEM] * len(scalars) + [given] * len(array...  21.6 us
    all_to_all x1, waiting for transfers between devices, on_device(): parts = lax.all_to_all(partial_sums, 'mp', 0, 0, tiled=True)  8.84 us
    psum x1, blocking collectives, on_device(): squares = lax.psum(jnp.sum(states * states, 1), 'mp')  8.77 us
    all_to_all x1, waiting for transfers between devices, spread(): return lax.all_to_all(copies, axis, 0, 0, tiled=True)  8.33 us
  transfers between devices with their start and end apart: 4, of which 3 were waited for; matrix products, arithmetic and copies ran while one was open for 2% of the time, Pallas kernels for 2%

profile of v2, /device:TPU:8, one launch (start us, length us, event | category | flops | bytes accessed | tf_op | source)
XLA Modules:
  0.0 243.9 jit_solution(18069633298767875027)
XLA Ops:
  9.4 3.7 %all_to_all.35 = bf16[2,8,1152]{2,1,0:T(8,128)(2,1)S(1)} all-to-all(bf16[2,8,1152]{2,1,0:T(8,128)(2,1)S(1)} %pad_maximum_fusion), channel_id=1, replica_groups=mesh['z'=8,'y'=8,'c'=2,'mp'=4] {'c'}, dimensions={0} | all-to-all | bytes 73728 | tf_op jit(solution)/shard_map/all_to_all | solution.py:356
  13.2 20.6 %all_to_all.36 = bf16[8,16,1152]{2,1,0:T(8,128)(2,1)} all-to-all(bf16[8,16,1152]{2,1,0:T(8,128)(2,1)S(1)} %broadcast_in_dim.73), channel_id=1, replica_groups=mesh['z'=8,'y'=8,'c'=2,'mp'=4] {'y'}, dimensions={0} | all-to-all | bytes 589824 | tf_op jit(solution)/shard_map/all_to_all | solution.py:323
  34.1 8.8 %psum.14 = f32[256]{0:T(256)S(1)} all-reduce(f32[256]{0:T(256)S(1)} %fusion), channel_id=1, replica_groups=mesh['z'=8,'y'=8,'c'=2,'mp'=4] {'mp'}, use_global_device_ids=true, to_apply=%region_2.3 | all-reduce | flops 256 | bytes 2048 | tf_op jit(solution)/shard_map/psum | solution.py:362
  44.2 33.5 %all-gather.2.cloned.1.call-done.weight_ref.w0 = bf16[1024,1152]{1,0:T(8,128)(2,1)} async-done(((bf16[128,1152]{1,0:T(8,128)(2,1)}), bf16[1024,1152]{1,0:T(8,128)(2,1)}) %all-gather.2.cloned.1.call-update) | async-done | bytes 2359312 | tf_op jit(solution)/shard_map/all_gather | solution.py:359
  77.8 1.9 collective-permute-start
  79.9 1.7 copy-done
  84.8 1.3 shard_map.112
  87.0 4.2 %all-to-all-start.2 = ((bf16[4,256,256]{2,1,0:T(8,128)(2,1)}), bf16[4,256,256]{2,1,0:T(8,128)(2,1)S(1)}, u32[]{:S(2)}, u32[]{:S(2)}) async-start(bf16[4,256,256]{2,1,0:T(8,128)(2,1)} %copy-done.10), calls=%async_computation.2 | async-start | bytes 1048576 | tf_op jit(solution)/shard_map/all_to_all | solution.py:374
  91.3 1.3 pad_add_fusion.1.slots_ref
  92.6 8.8 %all-to-all-done.2.parts_ref = bf16[4,256,256]{2,1,0:T(8,128)(2,1)S(1)} async-done(((bf16[4,256,256]{2,1,0:T(8,128)(2,1)}), bf16[4,256,256]{2,1,0:T(8,128)(2,1)S(1)}, u32[]{:S(2)}, u32[]{:S(2)}) %all-to-all-start.2) | async-done | bytes 524320 | tf_op jit(solution)/shard_map/all_to_all | solution.py:374
  102.2 2.2 shard_map.113
  104.4 42.5 %all_to_all.37.arrived_hbm = bf16[128,16,256]{2,1,0:T(8,128)(2,1)} all-to-all(bf16[128,16,256]{2,1,0:T(8,128)(2,1)} %get-tuple-element.26), channel_id=1, replica_groups=mesh['z'=8,'y'=8,'c'=2,'mp'=4] {'z','y','c'}, dimensions={0} | all-to-all | bytes 2097152 | tf_op jit(solution)/shard_map/all_to_all | solution.py:391
  146.9 10.5 %shard_map.114 = (f32[256,1024]{1,0:T(8,128)}, f32[256,256]{1,0:T(8,128)}, bf16[128,16,256]{2,1,0:T(8,128)(2,1)}) custom-call(s32[66]{0:T(128)} %pad_add_fusion.1.slots_ref, bf16[128,16,256]{2,1,0:T(8,128)(2,1)} %all_to_all.37.arrived_hbm, bf16[256,1024]{1,0:T(8,128)(2,1)} %query_hbm.1, bf16[256,1024]{1,0:T(8,128)(2,1)} %grad_hbm.1, bf16[256,256]{1,0:T(8,128)(2,1)} %self_hbm.1), custom_call_target="tpu_custom_call" | custom-call | flops 2147483648 | bytes 5242880 | tf_op jit(solution)/shard_map/pallas_call | solution.py:41
  157.4 37.5 %all_to_all.38.returned_ref = bf16[128,16,256]{2,1,0:T(8,128)(2,1)S(1)} all-to-all(bf16[128,16,256]{2,1,0:T(8,128)(2,1)} %get-tuple-element.27), channel_id=1, replica_groups=mesh['z'=8,'y'=8,'c'=2,'mp'=4] {'z','y','c'}, dimensions={0} | all-to-all | bytes 2097152 | tf_op jit(solution)/shard_map/all_to_all | solution.py:395
  195.0 1.6 shard_map.115
  196.6 12.1 %all_to_all.39.all_heads_ref = bf16[4,272,256]{2,1,0:T(8,128)(2,1)S(1)} all-to-all(bf16[4,272,256]{2,1,0:T(8,128)(2,1)S(1)} %broadcast_in_dim.77), channel_id=1, replica_groups=mesh['z'=8,'y'=8,'c'=2,'mp'=4] {'mp'}, dimensions={0} | all-to-all | bytes 1114112 | tf_op jit(solution)/shard_map/all_to_all | solution.py:323
  208.7 1.8 shard_map.117
  210.6 3.1 %psum.15 = bf16[16,128]{1,0:T(8,128)(2,1)} all-reduce(f32[16,128]{1,0:T(8,128)S(1)} %bitcast.16), channel_id=1, replica_groups=mesh['z'=8,'y'=8,'c'=2,'mp'=4] {'c'}, use_global_device_ids=true, to_apply=%region_4.5 | all-reduce | flops 2048 | bytes 12288 | tf_op jit(solution)/shard_map/psum | solution.py:416
  213.6 1.4 broadcast_in_dim.79
  215.1 5.8 %all-to-all-start.6 = ((bf16[64,16,128]{2,1,0:T(8,128)(2,1)}), bf16[64,16,128]{2,1,0:T(8,128)(2,1)}, u32[]{:S(2)}, u32[]{:S(2)}) async-start(bf16[64,16,128]{2,1,0:T(8,128)(2,1)} %broadcast_in_dim.79), calls=%async_computation.6 | async-start | bytes 524288 | tf_op jit(solution)/shard_map/all_to_all | solution.py:323
  220.9 1.7 copy-done.4
  224.2 2.9 %shard_map.116 = bf16[256,2048]{1,0:T(8,128)(2,1)} custom-call(s32[2]{0:T(128)S(1)} %copy-done.15, bf16[4,272,256]{2,1,0:T(8,128)(2,1)S(1)} %copy-done.9, bf16[1024,1152]{1,0:T(8,128)(2,1)S(1)} %copy-done.1, bf16[1024,1152]{1,0:T(8,128)(2,1)S(1)} %copy-done.4, bf16[256,2048]{1,0:T(8,128)(2,1)S(1)} %copy-done.5, f32[256,128]{1,0:T(8,128)S(1)} %broadcast_in_dim.74.inverse_ref, ...), custom_call_target="tpu_custom_call" | custom-call | flops 1073741824 | bytes 7340032 | tf_op jit(solution)/shard_map/pallas_call | solution.py:41
  227.1 8.3 %all-to-all-done.6 = bf16[64,16,128]{2,1,0:T(8,128)(2,1)} async-done(((bf16[64,16,128]{2,1,0:T(8,128)(2,1)}), bf16[64,16,128]{2,1,0:T(8,128)(2,1)}, u32[]{:S(2)}, u32[]{:S(2)}) %all-to-all-start.6) | async-done | bytes 262176 | tf_op jit(solution)/shard_map/all_to_all | solution.py:323
  235.5 1.6 convert_reduce_fusion
  (61 shorter events, 10.7 us)
Async XLA Ops:
  7.2 26.7 %copy-start.5 = (bf16[256,2048]{1,0:T(8,128)(2,1)S(1)}, bf16[256,2048]{1,0:T(8,128)(2,1)}, u32[]{:S(2)}) copy-start(bf16[256,2048]{1,0:T(8,128)(2,1)} %states_ref.1) | copy-start | bytes 3145732
  7.2 35.7 %copy-start.12 = (f32[2048]{0:T(1024)S(1)}, f32[2048]{0:T(1024)}, u32[]{:S(2)}) copy-start(f32[2048]{0:T(1024)} %param.9) | copy-start | bytes 24580
  7.2 70.5 %all-gather.2.cloned.1.call-start = ((), (), s32[]{:S(2)}) async-start(), calls=%async_computation.7 | async-start | bytes 2654208 | tf_op jit(solution)/shard_map/all_gather | solution.py:359
  8.1 0.5 copy-start.19
  77.8 7.0 %collective-permute-start = (bf16[1024,1152]{1,0:T(8,128)(2,1)}, bf16[1024,1152]{1,0:T(8,128)(2,1)S(1)}, u32[]{:S(2)}, u32[]{:S(2)}) collective-permute-start(bf16[1024,1152]{1,0:T(8,128)(2,1)} %all-gather.2.cloned.1.call-done.weight_ref.w0), channel_id=1, source_target_pairs={{0,4},{4,0},{1,5},{5,1},{2,6},{6,2},{3,7},{7,3},{8,12},{12,8},{9,1... | collective-permute-start | bytes 7077896 | tf_op jit(solution)/shard_map/ppermute | solution.py:368
  79.8 4.3 %copy-start.13 = (s32[2]{0:T(128)}, s32[2]{0:T(128)S(1)}, u32[]{:S(2)}) copy-start(s32[2]{0:T(128)S(1)} %pad_add_fusion.place_ref) | copy-start | bytes 28
  79.9 1.7 copy-start
  81.6 1.2 copy-start.6
  82.8 2.0 copy-start.7
  84.8 6.5 %copy-start.18 = (s32[2]{0:T(128)S(1)}, s32[2]{0:T(128)}, u32[]{:S(2)}) copy-start(s32[2]{0:T(128)} %param.15) | copy-start | bytes 28
  84.8 1.4 copy-start.2
  86.2 0.8 copy-start.10
  87.0 14.4 %all-to-all-start.2 = ((bf16[4,256,256]{2,1,0:T(8,128)(2,1)}), bf16[4,256,256]{2,1,0:T(8,128)(2,1)S(1)}, u32[]{:S(2)}, u32[]{:S(2)}) async-start(bf16[4,256,256]{2,1,0:T(8,128)(2,1)} %copy-done.10), calls=%async_computation.2 | async-start | bytes 1048576 | tf_op jit(solution)/shard_map/all_to_all | solution.py:374
  101.4 0.8 copy-start.17
  157.4 37.5 %copy-start.11 = (f32[16,16,256]{2,1,0:T(8,128)S(1)}, f32[16,16,256]{2,1,0:T(8,128)}, u32[]{:S(2)}) copy-start(f32[16,16,256]{2,1,0:T(8,128)} %get-tuple-element.28.keyvals_ref) | copy-start | bytes 786436
  157.4 37.5 %copy-start.16 = (s32[128]{0:T(128)S(1)}, s32[128]{0:T(128)}, u32[]{:S(2)}) copy-start(s32[128]{0:T(128)} %broadcast_add_fusion.wanted_ref) | copy-start | bytes 1540
  157.4 51.3 %copy-start.3 = (bf16[1024,1152]{1,0:T(8,128)(2,1)S(1)}, bf16[1024,1152]{1,0:T(8,128)(2,1)}, u32[]{:S(2)}) copy-start(bf16[1024,1152]{1,0:T(8,128)(2,1)} %copy-done.2) | copy-start | bytes 7077892
  194.9 13.7 %copy-start.1 = (bf16[1024,1152]{1,0:T(8,128)(2,1)S(1)}, bf16[1024,1152]{1,0:T(8,128)(2,1)}, u32[]{:S(2)}) copy-start(bf16[1024,1152]{1,0:T(8,128)(2,1)} %all-gather.2.cloned.1.call-done.weight_ref.w0) | copy-start | bytes 7077892
  194.9 13.7 %copy-start.14 = (s32[2]{0:T(128)S(1)}, s32[2]{0:T(128)}, u32[]{:S(2)}) copy-start(s32[2]{0:T(128)} %copy-done.13) | copy-start | bytes 28
  208.7 1.9 copy-start.8
  215.1 20.4 %all-to-all-start.6 = ((bf16[64,16,128]{2,1,0:T(8,128)(2,1)}), bf16[64,16,128]{2,1,0:T(8,128)(2,1)}, u32[]{:S(2)}, u32[]{:S(2)}) async-start(bf16[64,16,128]{2,1,0:T(8,128)(2,1)} %broadcast_in_dim.79), calls=%async_computation.6 | async-start | bytes 524288 | tf_op jit(solution)/shard_map/all_to_all | solution.py:323
  220.9 1.7 copy-start.4
  222.6 1.1 copy-start.9
  223.6 0.6 copy-start.15
Sparse Core Ops, SparseCore 0:
  34.0 43.7 all-gather.1

commit v3 on v2

--- a/solution.py
+++ b/solution.py
@@ -351,12 +351,10 @@
     turned = proj_weight.T
     columns = turned.shape[0]
     halves = jnp.transpose(turned.reshape(columns, 2, half), (1, 0, 2))
-    ridden = jnp.broadcast_to(requests[None, None], (2, columns, N_WIDE))
-    blob = jnp.concatenate([halves, ridden], axis=2)
-    blob = lax.all_to_all(blob, "c", 0, 0, tiled=True).reshape(2 * columns, half + N_WIDE)
-    blob = spread(blob, "y").reshape(-1, half + N_WIDE)
-    blob, passage_states = lax.optimization_barrier((blob, passage_states))
-    blob = lax.all_gather(blob, "z", axis=0, tiled=True)
+    block = lax.all_to_all(halves, "c", 0, 0, tiled=True).reshape(2 * columns, half)
+    ridden = jnp.broadcast_to(requests[None], (2 * columns, N_WIDE))
+    blob = jnp.concatenate([block, ridden], axis=1)
+    blob = spread(blob, ("z", "y")).reshape(-1, half + N_WIDE)
 
     states = passage_states.astype(jnp.float32)
     squares = lax.psum(jnp.sum(states * states, 1), "mp")
@@ -368,10 +366,15 @@
     other_weight = lax.ppermute(weight, "c", SWAP)
     own_sums = project(place, memory_rows, weight, jnp.float32)
     partial_sums = project(place[::-1], memory_rows, other_weight, jnp.bfloat16, own_sums)
-    wanted = weight.reshape(N_WIDE, columns, -1)[:, 0, half:].astype(jnp.int32)
-    wanted = jnp.sum(jnp.where(jnp.arange(N_WIDE)[None, :] == me, wanted, 0), 1) - 1
-    partial_sums, wanted = lax.optimization_barrier((partial_sums, wanted))
+    wanted = []
+    for tables in (weight, other_weight):
+        tables = tables.reshape(-1, 2 * columns, half + N_WIDE)[:, 0, half:].astype(jnp.int32)
+        wanted.append(jnp.sum(jnp.where(jnp.arange(N_WIDE)[None, :] == me, tables, 0), 1) - 1)
+    ours, theirs = wanted
+    wanted = jnp.where(core == 0, jnp.stack([ours, theirs], 1), jnp.stack([theirs, ours], 1))
+    wanted = wanted.reshape(-1)
     parts = lax.all_to_all(partial_sums, "mp", 0, 0, tiled=True)
+    parts, wanted = lax.optimization_barrier((parts, wanted))
     table = (P_DEV, MROWS, 2 * HEAD)
     outgoing, keyvals = kernel_call(
         pack_kernel,

time: 245 us -> 246 us (level)
  the two profiles are of different devices: /device:TPU:8 before, /device:TPU:2 now
where the time goes in v3:
time: 246 us; the launch traced here: 244 us
  blocking collectives  104 us (42%)
  waiting for transfers between devices  64.2 us (26%)
  starting transfers between devices  32.6 us (13%)
  Pallas kernels  25.2 us (10%)
  local copies, waits for them, and re-layouts  9.9 us (4%)
  other arithmetic  7.73 us (3%)
    all_to_all x2, waiting for transfers between devices, spread(): return lax.all_to_all(copies, axis, 0, 0, tiled=True)  59 us
    all_to_all x1, blocking collectives, on_device(): arrived = lax.all_to_all(outgoing, WIDE, 0, 0, tiled=True)  41.6 us
    all_to_all x1, blocking collectives, on_device(): returned = lax.all_to_all(memory_grads, WIDE, 0, 0, tiled=True)  37.5 us
    pallas_call x7, Pallas kernels, kernel_call(): pl.pallas_call(body, in_specs=[SMEM] * len(scalars) + [given] * len(array...  25.2 us
    all_to_all x2, starting transfers between devices, spread(): return lax.all_to_all(copies, axis, 0, 0, tiled=True)  22.6 us
    all_to_all x1, blocking collectives, spread(): return lax.all_to_all(copies, axis, 0, 0, tiled=True)  12.8 us
    psum x1, blocking collectives, on_device(): squares = lax.psum(jnp.sum(states * states, 1), 'mp')  8.62 us
  transfers between devices with their start and end apart: 5, of which 4 were waited for; matrix products, arithmetic and copies ran while one was open for 4% of the time, Pallas kernels for 2%

profile of v3, /device:TPU:2, one launch (start us, length us, event | category | flops | bytes accessed | tf_op | source)
XLA Modules:
  0.0 244.2 jit_solution(16358945481484026299)
XLA Ops:
  0.6 3.3 %all-to-all-start = ((bf16[2,8,1024]{2,1,0:T(8,128)(2,1)}), bf16[2,8,1024]{2,1,0:T(8,128)(2,1)S(1)}, u32[]{:S(2)}, u32[]{:S(2)}) async-start(bf16[2,8,1024]{2,1,0:T(8,128)(2,1)} %bitcast.32), calls=%async_computation | async-start | bytes 65536 | tf_op jit(solution)/shard_map/all_to_all | solution.py:354
  5.3 1.6 broadcast_in_dim.74
  6.9 16.7 %all-to-all-start.1 = ((bf16[64,16,1152]{2,1,0:T(8,128)(2,1)}), bf16[64,16,1152]{2,1,0:T(8,128)(2,1)S(1)}, u32[]{:S(2)}, u32[]{:S(2)}) async-start(bf16[64,16,1152]{2,1,0:T(8,128)(2,1)} %broadcast_in_dim.74), calls=%async_computation.1 | async-start | bytes 4718592 | tf_op jit(solution)/shard_map/all_to_all | solution.py:323
  23.9 8.6 %psum.14 = f32[256]{0:T(256)S(1)} all-reduce(f32[256]{0:T(256)S(1)} %fusion), channel_id=1, replica_groups=mesh['z'=8,'y'=8,'c'=2,'mp'=4] {'mp'}, use_global_device_ids=true, to_apply=%region_2.3 | all-reduce | flops 256 | bytes 2048 | tf_op jit(solution)/shard_map/psum | solution.py:360
  32.5 1.3 fusion.2.rows_ref
  33.8 49.7 %all-to-all-done.1 = bf16[64,16,1152]{2,1,0:T(8,128)(2,1)S(1)} async-done(((bf16[64,16,1152]{2,1,0:T(8,128)(2,1)}), bf16[64,16,1152]{2,1,0:T(8,128)(2,1)S(1)}, u32[]{:S(2)}, u32[]{:S(2)}) %all-to-all-start.1) | async-done | bytes 2359328 | tf_op jit(solution)/shard_map/all_to_all | solution.py:323
  83.6 1.9 collective-permute-start
  90.6 2.4 shard_map.112
  93.9 4.8 %all-to-all-start.2 = ((bf16[4,256,256]{2,1,0:T(8,128)(2,1)}), bf16[4,256,256]{2,1,0:T(8,128)(2,1)}, u32[]{:S(2)}, u32[]{:S(2)}) async-start(bf16[4,256,256]{2,1,0:T(8,128)(2,1)} %copy-done.5), calls=%async_computation.2 | async-start | bytes 1048576 | tf_op jit(solution)/shard_map/all_to_all | solution.py:376
  101.3 1.4 select_n.51.wanted_ref
  102.7 4.9 %all-to-all-done.2.parts_ref = bf16[4,256,256]{2,1,0:T(8,128)(2,1)} async-done(((bf16[4,256,256]{2,1,0:T(8,128)(2,1)}), bf16[4,256,256]{2,1,0:T(8,128)(2,1)}, u32[]{:S(2)}, u32[]{:S(2)}) %all-to-all-start.2) | async-done | bytes 524320 | tf_op jit(solution)/shard_map/all_to_all | solution.py:376
  107.6 2.2 shard_map.113
  109.8 41.6 %all_to_all.35.arrived_hbm = bf16[128,16,256]{2,1,0:T(8,128)(2,1)} all-to-all(bf16[128,16,256]{2,1,0:T(8,128)(2,1)} %get-tuple-element.22), channel_id=1, replica_groups=mesh['z'=8,'y'=8,'c'=2,'mp'=4] {'z','y','c'}, dimensions={0} | all-to-all | bytes 2097152 | tf_op jit(solution)/shard_map/all_to_all | solution.py:394
  151.4 10.5 %shard_map.114 = (f32[256,1024]{1,0:T(8,128)}, f32[256,256]{1,0:T(8,128)}, bf16[128,16,256]{2,1,0:T(8,128)(2,1)}) custom-call(s32[66]{0:T(128)} %pad_add_fusion.1.slots_ref, bf16[128,16,256]{2,1,0:T(8,128)(2,1)} %all_to_all.35.arrived_hbm, bf16[256,1024]{1,0:T(8,128)(2,1)} %query_hbm.1, bf16[256,1024]{1,0:T(8,128)(2,1)} %grad_hbm.1, bf16[256,256]{1,0:T(8,128)(2,1)} %self_hbm.1), custom_call_target="tpu_custom_call" | custom-call | flops 2147483648 | bytes 5242880 | tf_op jit(solution)/shard_map/pallas_call | solution.py:41
  161.9 37.5 %all_to_all.36.returned_ref = bf16[128,16,256]{2,1,0:T(8,128)(2,1)S(1)} all-to-all(bf16[128,16,256]{2,1,0:T(8,128)(2,1)} %get-tuple-element.23), channel_id=1, replica_groups=mesh['z'=8,'y'=8,'c'=2,'mp'=4] {'z','y','c'}, dimensions={0} | all-to-all | bytes 2097152 | tf_op jit(solution)/shard_map/all_to_all | solution.py:398
  199.4 1.6 shard_map.115
  201.1 12.8 %all_to_all.37.all_heads_ref = bf16[4,272,256]{2,1,0:T(8,128)(2,1)S(1)} all-to-all(bf16[4,272,256]{2,1,0:T(8,128)(2,1)S(1)} %broadcast_in_dim.77), channel_id=1, replica_groups=mesh['z'=8,'y'=8,'c'=2,'mp'=4] {'mp'}, dimensions={0} | all-to-all | bytes 1114112 | tf_op jit(solution)/shard_map/all_to_all | solution.py:323
  213.9 3.2 %shard_map.117 = f32[1,2048]{1,0:T(1,128)S(1)} custom-call(s32[2]{0:T(128)S(1)} %copy-done.9, bf16[4,272,256]{2,1,0:T(8,128)(2,1)S(1)} %all_to_all.37.all_heads_ref, bf16[1024,1152]{1,0:T(8,128)(2,1)S(1)} %bitcast.26, bf16[1024,1152]{1,0:T(8,128)(2,1)} %collective-permute-done.weight_ref.w1, bf16[256,2048]{1,0:T(8,128)(2,1)S(1)} %copy-done, ...), custom_call_target="tpu_custom_call" | custom-call | flops 1073741824 | bytes 6291456 | tf_op jit(solution)/shard_map/pallas_call | solution.py:41
  217.1 3.1 %psum.15 = bf16[16,128]{1,0:T(8,128)(2,1)} all-reduce(f32[16,128]{1,0:T(8,128)S(1)} %bitcast.29), channel_id=1, replica_groups=mesh['z'=8,'y'=8,'c'=2,'mp'=4] {'c'}, use_global_device_ids=true, to_apply=%region_5.6 | all-reduce | flops 2048 | bytes 12288 | tf_op jit(solution)/shard_map/psum | solution.py:419
  220.2 1.4 broadcast_in_dim.79
  221.6 5.8 %all-to-all-start.6 = ((bf16[64,16,128]{2,1,0:T(8,128)(2,1)}), bf16[64,16,128]{2,1,0:T(8,128)(2,1)}, u32[]{:S(2)}, u32[]{:S(2)}) async-start(bf16[64,16,128]{2,1,0:T(8,128)(2,1)} %broadcast_in_dim.79), calls=%async_computation.6 | async-start | bytes 524288 | tf_op jit(solution)/shard_map/all_to_all | solution.py:323
  229.2 4.1 %shard_map.116 = bf16[256,2048]{1,0:T(8,128)(2,1)} custom-call(s32[2]{0:T(128)S(1)} %copy-done.10, bf16[4,272,256]{2,1,0:T(8,128)(2,1)S(1)} %copy-done.4, bf16[1024,1152]{1,0:T(8,128)(2,1)S(1)} %bitcast.27, bf16[1024,1152]{1,0:T(8,128)(2,1)} %collective-permute-done.weight_ref.w1, bf16[256,2048]{1,0:T(8,128)(2,1)S(1)} %copy-done, ...), custom_call_target="tpu_custom_call" | custom-call | flops 1073741824 | bytes 7340032 | tf_op jit(solution)/shard_map/pallas_call | solution.py:41
  233.3 9.3 %all-to-all-done.6 = bf16[64,16,128]{2,1,0:T(8,128)(2,1)} async-done(((bf16[64,16,128]{2,1,0:T(8,128)(2,1)}), bf16[64,16,128]{2,1,0:T(8,128)(2,1)}, u32[]{:S(2)}, u32[]{:S(2)}) %all-to-all-start.6) | async-done | bytes 262176 | tf_op jit(solution)/shard_map/all_to_all | solution.py:323
  242.6 1.6 convert_reduce_fusion
  (52 shorter events, 11.9 us)
Async XLA Ops:
  0.6 4.7 %all-to-all-start = ((bf16[2,8,1024]{2,1,0:T(8,128)(2,1)}), bf16[2,8,1024]{2,1,0:T(8,128)(2,1)S(1)}, u32[]{:S(2)}, u32[]{:S(2)}) async-start(bf16[2,8,1024]{2,1,0:T(8,128)(2,1)} %bitcast.32), calls=%async_computation | async-start | bytes 65536 | tf_op jit(solution)/shard_map/all_to_all | solution.py:354
  4.7 0.5 copy-start.13
  6.9 16.7 %copy-start = (bf16[256,2048]{1,0:T(8,128)(2,1)S(1)}, bf16[256,2048]{1,0:T(8,128)(2,1)}, u32[]{:S(2)}) copy-start(bf16[256,2048]{1,0:T(8,128)(2,1)} %states_ref.3) | copy-start | bytes 3145732
  6.9 25.7 %copy-start.7 = (f32[2048]{0:T(1024)S(1)}, f32[2048]{0:T(1024)}, u32[]{:S(2)}) copy-start(f32[2048]{0:T(1024)} %param.9) | copy-start | bytes 24580
  6.9 76.6 %all-to-all-start.1 = ((bf16[64,16,1152]{2,1,0:T(8,128)(2,1)}), bf16[64,16,1152]{2,1,0:T(8,128)(2,1)S(1)}, u32[]{:S(2)}, u32[]{:S(2)}) async-start(bf16[64,16,1152]{2,1,0:T(8,128)(2,1)} %broadcast_in_dim.74), calls=%async_computation.1 | async-start | bytes 4718592 | tf_op jit(solution)/shard_map/all_to_all | solution.py:323
  83.6 7.1 %collective-permute-start = (bf16[1024,1152]{1,0:T(8,128)(2,1)S(1)}, bf16[1024,1152]{1,0:T(8,128)(2,1)}, u32[]{:S(2)}, u32[]{:S(2)}) collective-permute-start(bf16[1024,1152]{1,0:T(8,128)(2,1)S(1)} %bitcast.24), channel_id=1, source_target_pairs={{0,4},{4,0},{1,5},{5,1},{2,6},{6,2},{3,7},{7,3},{8,12},{12,8},{9,1... | collective-permute-start | bytes 7077896 | tf_op jit(solution)/shard_map/ppermute | solution.py:366
  85.6 5.0 %copy-start.8 = (s32[2]{0:T(128)}, s32[2]{0:T(128)S(1)}, u32[]{:S(2)}) copy-start(s32[2]{0:T(128)S(1)} %pad_add_fusion.place_ref) | copy-start | bytes 28
  88.1 1.2 copy-start.1
  89.3 1.3 copy-start.2
  90.6 9.0 %copy-start.12 = (pred[128]{0:T(512)(128)(4,1)S(1)}, pred[128]{0:T(512)(128)(4,1)}, u32[]{:S(2)}) copy-start(pred[128]{0:T(512)(128)(4,1)} %iota_compare_fusion.2) | copy-start | bytes 388
  93.1 0.8 copy-start.5
  93.9 13.7 %all-to-all-start.2 = ((bf16[4,256,256]{2,1,0:T(8,128)(2,1)}), bf16[4,256,256]{2,1,0:T(8,128)(2,1)}, u32[]{:S(2)}, u32[]{:S(2)}) async-start(bf16[4,256,256]{2,1,0:T(8,128)(2,1)} %copy-done.5), calls=%async_computation.2 | async-start | bytes 1048576 | tf_op jit(solution)/shard_map/all_to_all | solution.py:376
  161.8 37.6 %copy-start.6 = (f32[16,16,256]{2,1,0:T(8,128)S(1)}, f32[16,16,256]{2,1,0:T(8,128)}, u32[]{:S(2)}) copy-start(f32[16,16,256]{2,1,0:T(8,128)} %get-tuple-element.24.keyvals_ref) | copy-start | bytes 786436
  161.8 37.6 %copy-start.11 = (s32[128]{0:T(128)S(1)}, s32[128]{0:T(128)}, u32[]{:S(2)}) copy-start(s32[128]{0:T(128)} %select_n.51.wanted_ref) | copy-start | bytes 1540
  199.4 14.5 %copy-start.9 = (s32[2]{0:T(128)S(1)}, s32[2]{0:T(128)}, u32[]{:S(2)}) copy-start(s32[2]{0:T(128)} %copy-done.8) | copy-start | bytes 28
  213.9 3.2 %copy-start.3 = (bf16[4,272,256]{2,1,0:T(8,128)(2,1)}, bf16[4,272,256]{2,1,0:T(8,128)(2,1)S(1)}, u32[]{:S(2)}) copy-start(bf16[4,272,256]{2,1,0:T(8,128)(2,1)S(1)} %all_to_all.37.all_heads_ref) | copy-start | bytes 1671172
  221.6 21.0 %all-to-all-start.6 = ((bf16[64,16,128]{2,1,0:T(8,128)(2,1)}), bf16[64,16,128]{2,1,0:T(8,128)(2,1)}, u32[]{:S(2)}, u32[]{:S(2)}) async-start(bf16[64,16,128]{2,1,0:T(8,128)(2,1)} %broadcast_in_dim.79), calls=%async_computation.6 | async-start | bytes 524288 | tf_op jit(solution)/shard_map/all_to_all | solution.py:323
  227.5 1.1 copy-start.4
  228.6 0.7 copy-start.10
